TPU v7x, 256 devices: a whole 4x4x8 slice. The times are simulated.
256 devices in a mesh: tok: 64 (over z, y, core), hid: 4 (over x).
Axes of the slice: x: 4, y: 4, z: 8, core: 2. Of those that a mesh axis runs over, the one named last changes fastest.
Arguments:
- tokens: bfloat16 [32768, 1024], P('tok', 'hid'), may hold values from -6 to 6
- width_index: int32 [32768], P('tok'), may hold values from 0 to 3, as said below
- up_weight: bfloat16 [1024, 4096], P('tok', 'hid'), may hold values from -0.1875 to 0.1875
- down_weight: bfloat16 [4096, 1024], P('hid', 'tok'), may hold values from -0.1875 to 0.1875
- cotangent: bfloat16 [32768, 1024], P('tok', 'hid'), may hold values from -6 to 6
Outputs:
- mixed: bfloat16 [32768, 1024], P('tok', 'hid')
- grad_tokens: bfloat16 [32768, 1024], P('tok', 'hid')
- grad_up: float32 [1024, 4096], P('tok', 'hid')
- grad_down: float32 [4096, 1024], P('hid', 'tok')
Inputs may be any that keep to these rules, and one draw needn't show every extreme that they name: `width_index`: on each index of tok (its 512 tokens), at most 256 tokens have width index 1 or more, at most 128 have 2 or more and at most 64 have 3; in every draw some index of tok holds exactly 256, 128 and 64 such tokens.
All inputs are finite; a program needn't handle non-finite values.
Results may differ from a plain program's by a relative error of at most 0.0049.
Values may be sent and summed in bfloat16 or wider, within the bound.
A program may use at most 128 MiB of HBM per device.

v0:
```python
from functools import partial

import jax
import jax.numpy as jnp
from jax import lax
from jax.sharding import PartitionSpec as P

root_half = 0.7071067811865476
inv_root_tau = 0.3989422804014327


def gelu_pair(pre_act):
    cumul = 0.5 * (1.0 + jax.scipy.special.erf(pre_act * root_half))
    return (pre_act * cumul, cumul + pre_act * jnp.exp(-0.5 * pre_act * pre_act) * inv_root_tau)


def piece_plans(unit_count):
    half_units = unit_count // 2
    return [
        [(0, half_units, 0), (half_units, unit_count, 1)],
        [(0, unit_count, 2)],
        [(0, unit_count, 3)],
        [(0, unit_count, 3)],
    ]


def local_pass(pieces, capacity, token_rows, grad_rows, width_rows, up_full, down_full):
    row_count = token_rows.shape[0]
    model_cols = token_rows.shape[1]
    unit_count = up_full.shape[1]
    out_sum = jnp.zeros((row_count, model_cols), jnp.float32)
    back_sum = jnp.zeros((row_count, model_cols), jnp.float32)
    hidden_all = jnp.zeros((row_count, unit_count), jnp.bfloat16)
    grad_all = jnp.zeros((row_count, unit_count), jnp.bfloat16)
    for col_lo, col_hi, least_index in pieces:
        row_cap = capacity[least_index]
        keep_mask = (width_rows[:row_cap] >= least_index)[:, None]
        pre_act = jnp.dot(
            token_rows[:row_cap], up_full[:, col_lo:col_hi], preferred_element_type=jnp.float32
        )
        act_value, act_slope = gelu_pair(pre_act)
        hidden = jnp.where(keep_mask, act_value, 0.0).astype(jnp.bfloat16)
        grad_hidden = jnp.einsum(
            "td,ud->tu",
            grad_rows[:row_cap],
            down_full[col_lo:col_hi],
            preferred_element_type=jnp.float32,
        )
        grad_pre = jnp.where(keep_mask, grad_hidden * act_slope, 0.0).astype(jnp.bfloat16)
        out_sum = out_sum.at[:row_cap].add(
            jnp.dot(hidden, down_full[col_lo:col_hi], preferred_element_type=jnp.float32)
        )
        back_sum = back_sum.at[:row_cap].add(
            jnp.einsum(
                "tu,du->td", grad_pre, up_full[:, col_lo:col_hi], preferred_element_type=jnp.float32
            )
        )
        hidden_all = hidden_all.at[:row_cap, col_lo:col_hi].set(hidden)
        grad_all = grad_all.at[:row_cap, col_lo:col_hi].set(grad_pre)
    return (out_sum, back_sum, hidden_all, grad_all)


def term_rows(pieces, capacity, token_rows, grad_rows, hidden_all, grad_all, first_row, row_total):
    up_parts = []
    down_parts = []
    for col_lo, col_hi, least_index in pieces:
        row_cap = capacity[least_index]
        token_cols = lax.dynamic_slice_in_dim(token_rows[:row_cap], first_row, row_total, 1)
        grad_cols = lax.dynamic_slice_in_dim(grad_rows[:row_cap], first_row, row_total, 1)
        up_parts.append(
            jnp.einsum(
                "tr,tu->ru",
                token_cols,
                grad_all[:row_cap, col_lo:col_hi],
                preferred_element_type=jnp.float32,
            )
        )
        down_parts.append(
            jnp.einsum(
                "tr,tu->ru",
                grad_cols,
                hidden_all[:row_cap, col_lo:col_hi],
                preferred_element_type=jnp.float32,
            )
        )
    return (jnp.concatenate(up_parts, axis=1), jnp.concatenate(down_parts, axis=1))


def per_device(tokens, width_index, up_weight, down_weight, cotangent):
    token_full, grad_full = (
        lax.all_gather(tokens, "hid", axis=1, tiled=True),
        lax.all_gather(cotangent, "hid", axis=1, tiled=True),
    )
    up_full = lax.all_gather(up_weight, "tok", axis=0, tiled=True)
    down_full = lax.all_gather(down_weight, "tok", axis=1, tiled=True)
    row_count = tokens.shape[0]
    unit_count = up_full.shape[1]
    pieces_all = piece_plans(unit_count)
    capacity = (row_count, row_count, row_count, row_count)
    hid_level = lax.axis_index("hid")
    branches = [
        partial(
            local_pass, pieces, capacity, token_full, grad_full, width_index, up_full, down_full
        )
        for pieces in pieces_all
    ]
    out_sum, back_sum, hidden_all, grad_all = lax.switch(hid_level, branches)
    out_part, back_part = (
        lax.psum_scatter(out_sum, "hid", scatter_dimension=1, tiled=True),
        lax.psum_scatter(back_sum, "hid", scatter_dimension=1, tiled=True),
    )
    mixed = out_part.astype(jnp.bfloat16)
    grad_tokens = back_part.astype(jnp.bfloat16)

    def both_terms(first_row, row_total):
        term_branches = [
            partial(
                term_rows,
                pieces,
                capacity,
                token_full,
                grad_full,
                hidden_all,
                grad_all,
                first_row,
                row_total,
            )
            for pieces in pieces_all
        ]
        return lax.switch(hid_level, term_branches)

    local_rows = up_weight.shape[0]
    grad_up = lax.psum_scatter(
        both_terms(jnp.int32(0), local_rows * lax.axis_size("tok"))[0],
        "tok",
        scatter_dimension=0,
        tiled=True,
    )
    grad_down = lax.psum_scatter(
        both_terms(jnp.int32(0), local_rows * lax.axis_size("tok"))[1],
        "tok",
        scatter_dimension=0,
        tiled=True,
    ).T
    return (mixed, grad_tokens, grad_up, grad_down)


def solution(mesh):
    placed = (P("tok", "hid"), P("tok"), P("tok", "hid"), P("hid", "tok"), P("tok", "hid"))
    return jax.shard_map(
        per_device,
        mesh=mesh,
        in_specs=placed,
        out_specs=(P("tok", "hid"), P("tok", "hid"), P("tok", "hid"), P("hid", "tok")),
        check_vma=False,
    )
```

profile of v0, /device:TPU:1, one launch (start us, length us, event | category | flops | bytes accessed | tf_op | source)
XLA Modules:
  0.0 611.0 jit_solution(10641251213928574463)
XLA Ops:
  7.2 0.7 all-gather.7.cloned.1.call-update
  7.9 0.7 all-gather.11.cloned.1.call-update
  8.6 0.0 all-gather.5.cloned.1.call-start
  8.7 0.7 all-gather.5.cloned.1.call-update
  9.4 0.0 all-gather.9.cloned.1.call-start
  9.4 0.5 all-gather.9.cloned.1.call-update
  10.0 0.0 reduce-scatter.5.cloned.1.call-start
  10.0 31.1 %all-gather.7.cloned.1.call-done = bf16[512,1024]{1,0:T(8,128)(2,1)} async-done(((bf16[512,256]{1,0:T(8,128)(2,1)}), bf16[512,1024]{1,0:T(8,128)(2,1)}) %all-gather.7.cloned.1.call-update) | async-done | bytes 1048592 | tf_op jit(solution)/shard_map/all_gather | solution.py:91
  41.2 31.2 %all-gather.11.cloned.1.call-done = bf16[512,1024]{1,0:T(8,128)(2,1)} async-done(((bf16[512,256]{1,0:T(8,128)(2,1)}), bf16[512,1024]{1,0:T(8,128)(2,1)}) %all-gather.11.cloned.1.call-update) | async-done | bytes 1048592 | tf_op jit(solution)/shard_map/all_gather | solution.py:92
  72.4 82.4 %all-gather.5.cloned.1.call-done = bf16[1024,1024]{1,0:T(8,128)(2,1)} async-done(((bf16[16,1024]{1,0:T(8,128)(2,1)}), bf16[1024,1024]{1,0:T(8,128)(2,1)}) %all-gather.5.cloned.1.call-update) | async-done | bytes 2097168 | tf_op jit(solution)/shard_map/all_gather | solution.py:94
  154.8 77.6 %all-gather.9.cloned.1.call-done = bf16[1024,1024]{0,1:T(8,128)(2,1)} async-done(((bf16[1024,16]{0,1:T(8,128)(2,1)}), bf16[1024,1024]{0,1:T(8,128)(2,1)}) %all-gather.9.cloned.1.call-update) | async-done | bytes 2097168 | tf_op jit(solution)/shard_map/all_gather | solution.py:95
  232.4 16.6 %conditional.3 = (f32[512,1024]{1,0:T(8,128)}, f32[512,1024]{1,0:T(8,128)S(1)}, bf16[512,1024]{0,1:T(8,128)(2,1)S(1)}, bf16[512,1024]{0,1:T(8,128)(2,1)}) conditional(s32[]{:T(128)} %clamp.2, (s32[512]{0:T(512)}, bf16[1024,1024]{1,0:T(8,128)(2,1)}, bf16[512,1024]{1,0:T(8,128)(2,1)}, bf16[1024,1024]{0,1:T(8,128)(2,1)}, ...), branch_computations={%region_0.2_spmd, %region_2.0_spmd, %region_3.0_spmd, %region_4.0_... | conditional | flops 4309648384 | bytes 59782292 | solution.py:107
  232.4 0.6 compare_reduce_fusion
  233.1 2.9 copy.44
  236.1 2.2 select_convert_fusion
  238.3 1.0 fusion.3
  239.3 0.5 copy-done.10
  239.9 1.6 broadcast_select_fusion.1
  241.4 1.7 broadcast_select_fusion
  243.2 1.1 pad_maximum_fusion
  244.3 0.7 fusion.15
  245.0 2.0 convolution_add_fusion.1
  247.1 0.8 fusion.20
  247.8 0.8 convolution_add_fusion
  249.1 1.0 copy-done.9
  250.0 0.0 reduce-scatter.7.cloned.1.call-start
  250.1 0.6 copy-done
  250.7 0.6 copy-done.3
  251.3 7.5 %conditional.5 = (f32[1024,1024]{0,1:T(8,128)}) conditional(s32[]{:T(128)} %clamp.2, (bf16[512,1024]{0,1:T(8,128)(2,1)}, bf16[512,1024]{1,0:T(8,128)(2,1)S(1)}) %tuple.254, (bf16[512,1024]{1,0:T(8,128)(2,1)S(1)}, bf16[512,1024]{0,1:T(8,128)(2,1)}) %tuple.255, (bf16[512,1024]{1,0:T(8,128)(2,1)S(1)}, ...), branch_computations={%region_12.13_spmd, %region_13.14_spmd, %region_14.15_spmd, %regio... | conditional | flops 1074790400 | bytes 22020132 | solution.py:130
  251.3 2.3 copy.53
  253.6 1.9 fusion.51
  255.5 0.7 fusion.49
  256.2 2.6 pad_maximum_fusion.3
  258.8 5.3 copy.57
  264.2 0.0 reduce-scatter.9.cloned.1.call-start
  264.2 1.2 copy-done.1
  265.4 5.6 conditional.4
  265.4 1.5 copy.48
  266.9 0.8 fusion.47
  267.7 0.8 fusion.45
  268.4 2.6 pad_maximum_fusion.2
  271.0 5.5 copy.52
  276.5 2.4 reduce-scatter.5.cloned.1.call-done
  278.9 1.8 convert_element_type.36
  280.7 32.8 %reduce-scatter.7.cloned.1.call-done = f32[512,256]{1,0:T(8,128)} async-done(((f32[512,1024]{1,0:T(8,128)}), f32[512,256]{1,0:T(8,128)}) %reduce-scatter.7.cloned.1.call-update) | async-done | bytes 524304 | tf_op jit(solution)/shard_map/reduce_scatter | solution.py:110
  313.5 1.8 convert_element_type.37
  315.2 141.5 %reduce-scatter.11.cloned.1.call-done = f32[16,1024]{1,0:T(8,128)} async-done(((f32[1024,1024]{1,0:T(8,128)}), f32[16,1024]{1,0:T(8,128)}) %reduce-scatter.11.cloned.1.call-update) | async-done | bytes 65552 | tf_op jit(solution)/shard_map/reduce_scatter | solution.py:139
  456.7 147.4 %reduce-scatter.9.cloned.1.call-done = f32[16,1024]{1,0:T(8,128)} async-done(((f32[1024,1024]{1,0:T(8,128)}), f32[16,1024]{1,0:T(8,128)}) %reduce-scatter.9.cloned.1.call-update) | async-done | bytes 65552 | tf_op jit(solution)/shard_map/reduce_scatter | solution.py:133
  (21 shorter events, 0.2 us)
Async XLA Ops:
  7.2 34.0 %all-gather.7.cloned.1.call-start = ((), (), s32[]{:S(2)}) async-start(), calls=%async_computation.5 | async-start | bytes 1310720 | tf_op jit(solution)/shard_map/all_gather | solution.py:91
  7.9 64.5 %all-gather.11.cloned.1.call-start = ((), (), s32[]{:S(2)}) async-start(), calls=%async_computation.7 | async-start | bytes 1310720 | tf_op jit(solution)/shard_map/all_gather | solution.py:92
  8.6 146.2 %all-gather.5.cloned.1.call-start = ((), (), s32[]{:S(2)}) async-start(), calls=%async_computation.4 | async-start | bytes 2129920 | tf_op jit(solution)/shard_map/all_gather | solution.py:94
  9.4 223.1 %all-gather.9.cloned.1.call-start = ((), (), s32[]{:S(2)}) async-start(), calls=%async_computation.6 | async-start | bytes 2129920 | tf_op jit(solution)/shard_map/all_gather | solution.py:95
  10.0 268.9 %reduce-scatter.5.cloned.1.call-start = ((), (), s32[]{:S(2)}) async-start(), calls=%async_computation.8 | async-start | bytes 2621440 | tf_op jit(solution)/shard_map/reduce_scatter | solution.py:109
  233.1 3.0 copy-start.14
  233.1 3.0 copy-start.2
  236.1 2.2 copy-start.4
  238.3 1.6 copy-start.10
  249.0 1.0 copy-start.9
  249.0 1.6 copy-start
  250.0 1.3 copy-start.3
  250.0 63.4 %reduce-scatter.7.cloned.1.call-start = ((), (), s32[]{:S(2)}) async-start(), calls=%async_computation.9 | async-start | bytes 2621440 | tf_op jit(solution)/shard_map/reduce_scatter | solution.py:110
  250.7 206.0 %reduce-scatter.11.cloned.1.call-start = ((), (), s32[]{:S(2)}) async-start(), calls=%async_computation.11 | async-start | bytes 4259840 | tf_op jit(solution)/shard_map/reduce_scatter | solution.py:139
  253.6 1.9 copy-start.8
  264.2 1.2 copy-start.1
  264.2 340.0 %reduce-scatter.9.cloned.1.call-start = ((), (), s32[]{:S(2)}) async-start(), calls=%async_computation.10 | async-start | bytes 4259840 | tf_op jit(solution)/shard_map/reduce_scatter | solution.py:133
Sparse Core Ops, SparseCore 0:
  9.8 31.3 all-gather.6
  43.0 29.3 all-gather.10
  75.2 79.6 all-gather.4
  157.4 74.9 all-gather.8
  250.2 28.6 reduce-scatter.4
  281.5 31.9 reduce-scatter.6
  318.2 138.5 reduce-scatter.10
  462.0 142.0 reduce-scatter.8
where the time goes:
time: 616 us; the launch traced here: 611 us
  waiting for transfers between devices  549 us (89%)
  local copies, waits for them, and re-layouts  21.4 us (3%)
  matrix products  14.9 us (2%)
  between operations  14.2 us (2%)
  other arithmetic  10.4 us (2%)
    reduce_scatter x2, waiting for transfers between devices, per_device(): lax.psum_scatter(both_terms(jnp.int32(0), local_rows * lax.axis_size('tok...  289 us
    all_gather x1, waiting for transfers between devices, per_device(): up_full = lax.all_gather(up_weight, 'tok', axis=0, tiled=True)  82.4 us
    all_gather x1, waiting for transfers between devices, per_device(): down_full = lax.all_gather(down_weight, 'tok', axis=1, tiled=True)  77.6 us
    reduce_scatter x1, waiting for transfers between devices, per_device(): lax.psum_scatter(back_sum, 'hid', scatter_dimension=1, tiled=True)  32.8 us
    all_gather x1, waiting for transfers between devices, per_device(): lax.all_gather(cotangent, 'hid', axis=1, tiled=True)  31.2 us
    all_gather x1, waiting for transfers between devices, per_device(): lax.all_gather(tokens, 'hid', axis=1, tiled=True)  31.1 us
  transfers between devices with their start and end apart: 8, of which 8 were waited for; matrix products, arithmetic and copies ran while one was open for 4% of the time, Pallas kernels for 0%

commit v1 on v0

v1 whole, which is shorter than its diff:
```python
import jax
import jax.numpy as jnp
from jax import lax
from jax.experimental import pallas as pl
from jax.experimental.pallas import tpu as pltpu
from jax.sharding import PartitionSpec as P

root_half = 0.7071067811865476
inv_root_tau = 0.3989422804014327
F32 = jnp.float32
BF16 = jnp.bfloat16
MESH = pl.DeviceIdType.MESH

ROWS = 512
COLS = 256
D = 1024
UNITS = 1024
NZ, NY = 8, 4
TILE = 256
N_SEM = 128

NT = (((1,), (1,)), ((), ()))
TN = (((0,), (0,)), ((), ()))


def gelu_pair(pre_act):
    cumul = 0.5 * (1.0 + lax.erf(pre_act * root_half))
    return (pre_act * cumul, cumul + pre_act * jnp.exp(-0.5 * pre_act * pre_act) * inv_root_tau)


def kernel(
    tok_ref, wid_ref, up_ref, down_ref, cot_ref,
    mixed_ref, gtok_ref, gup_ref, gdown_ref,
    uf, vf, xg, hbuf, pbuf, so, ro, fo, perm, permt,
    gsend, grecv, lane,
    sv, rv, su0, ru0, su1, ru1, suz, ruz, svy0, rvy0, svy1, rvy1, uy, vz,
    ssem, rsem,
):
    hid = lax.axis_index("hid")
    tok = lax.axis_index("tok")
    c = lax.rem(tok, 2)
    y = lax.rem(lax.div(tok, 2), NY)
    z = lax.div(tok, 2 * NY)

    def zmod(v):
        return lax.rem(v + 2 * NZ, NZ)

    def ymod(v):
        return lax.rem(v + 2 * NY, NY)

    def at(zz, yy, cc):
        return {"tok": (zz * NY + yy) * 2 + cc}

    zp, zm = at(zmod(z + 1), y, c), at(zmod(z - 1), y, c)
    yp, ym = at(z, ymod(y + 1), c), at(z, ymod(y - 1), c)
    mate = at(z, y, 1 - c)
    near = (zp, zm, yp, ym, mate)
    xs = [{"hid": lax.rem(hid + k, 4)} for k in (1, 2, 3)]

    slots = {}
    sent = []

    def msg(key, src, dst, dev):
        if key not in slots:
            slots[key] = len(slots)
        i = slots[key]
        return pltpu.make_async_remote_copy(
            src_ref=src, dst_ref=dst, send_sem=ssem.at[i], recv_sem=rsem.at[i],
            device_id=dev, device_id_type=MESH,
        )

    def send(key, src, dst, dev, plane=None, again=None):
        msg(key, src, dst, dev).start()
        sent.append((key, again or (lambda: src), plane))

    def recv(key, dst):
        msg(key, dst, dst, mate).wait_recv()

    barrier = pltpu.get_barrier_semaphore()
    for dev in near + tuple(xs):
        pl.semaphore_signal(barrier, inc=1, device_id=dev, device_id_type=MESH)

    uf[z, y, c] = up_ref[...]
    vf[z, y, c] = down_ref[...]

    pl.semaphore_wait(barrier, len(near) + len(xs))

    y1, y3, y2 = ymod(y + 1), ymod(y - 1), ymod(y + 2)

    def u_z(direction, s):
        zz = zmod(z - s) if direction == 0 else zmod(z + s)
        send(("uz", direction, s), uf.at[zz, y, c], uf.at[zz, y, c], zp if direction == 0 else zm)

    def u_z_recv(direction, s):
        recv(("uz", direction, s), uf.at[z, y, c])

    def u_y(i, zz):
        for k, dev in ((0, yp), (1, ym)):
            send(("uy", i, k), uf.at[zz, y, c], uf.at[zz, y, c], dev)

    def u_y_recv(i, zz):
        recv(("uy", i, 0), uf.at[zz, y3, c])
        recv(("uy", i, 1), uf.at[zz, y1, c])
        if i % 2 == 0:
            send(("uyf", i), uf.at[zz, y3, c], uf.at[zz, y3, c], yp)
        else:
            send(("uyf", i), uf.at[zz, y1, c], uf.at[zz, y1, c], ym)

    def v_z(direction, half, s):
        zz = zmod(z - s) if direction == 0 else zmod(z + s)
        ref = vf.at[zz, pl.ds(2 * half, 2), c]
        send(("vz", direction, half, s), ref, ref, zp if direction == 0 else zm)

    def v_z_recv(direction, half, s):
        recv(("vz", direction, half, s), vf.at[z, pl.ds(2 * half, 2), c])

    order = [(None, 0), (0, 0), (1, 0), (0, 1), (1, 1), (0, 2), (1, 2), (0, 3)]
    z_of = [z] + [zmod(z - s - 1) if d == 0 else zmod(z + s + 1) for d, s in order[1:]]

    send(("vy", 0), vf.at[z, y, c], vf.at[z, y, c], yp)
    send(("vy", 1), vf.at[z, y, c], vf.at[z, y, c], ym)
    u_z(0, 0)
    u_z(1, 0)
    u_y(0, z)

    wid = wid_ref[...]
    level = lax.broadcasted_iota(jnp.int32, (8, ROWS), 0)
    ind = (jnp.broadcast_to(wid, (8, ROWS)) == level).astype(F32)
    ind16 = ind.astype(BF16)
    ia = lax.broadcasted_iota(jnp.int32, (ROWS, ROWS), 0)
    ib = lax.broadcasted_iota(jnp.int32, (ROWS, ROWS), 1)
    above = (ia < ib).astype(F32).astype(BF16)
    below = (ib < ia).astype(F32).astype(BF16)
    eye = (ia == ib).astype(F32).astype(BF16)
    counts = jnp.sum(ind, axis=1, keepdims=True)
    wider = [
        sum([counts[k:k + 1] for k in range(lo, 4)], jnp.zeros((1, 1), F32)) for lo in range(5)
    ]
    pre_row = jnp.dot(ind16, above, preferred_element_type=F32)
    pre_col = lax.dot_general(below, ind16, NT, preferred_element_type=F32)
    ind_col = lax.dot_general(eye, ind16, NT, preferred_element_type=F32)
    rank_row = sum([ind[k:k + 1] * (pre_row[k:k + 1] + wider[k + 1]) for k in range(4)])
    rank_col = sum(
        [ind_col[:, k:k + 1] * (pre_col[:, k:k + 1] + wider[k + 1]) for k in range(4)]
    )
    perm[...] = (ia == rank_row.astype(jnp.int32)).astype(F32).astype(BF16)
    permt[...] = (ib == rank_col.astype(jnp.int32)).astype(F32).astype(BF16)
    mine = pl.ds(pl.multiple_of(hid * COLS, COLS), COLS)
    for a, ref in ((0, tok_ref), (1, cot_ref)):
        xg[a, :, mine] = jnp.dot(perm[...], ref[...], preferred_element_type=F32).astype(BF16)

    def xpart(h, lo, hi):
        return xg.at[:, pl.ds(lo, hi - lo), pl.ds(h * COLS, COLS)]

    def xsend(src, dst, h, lo, hi):
        part = xpart(h, lo, hi)
        send(("x", src, dst, h, lo), part, part, xs[(dst - src) % 4 - 1], src,
             lambda: xpart(h, lo, hi))

    def xrecv(src, dst, h, lo, hi):
        recv(("x", src, dst, h, lo), xpart(h, lo, hi))

    @pl.when(hid == 2)
    def _():
        xsend(2, 1, 2, 0, 128)
        xsend(2, 3, 2, 128, 256)
        xsend(2, 3, 2, 0, 64)
        xsend(2, 1, 2, 256, 384)
        xsend(2, 3, 2, 384, 512)

    @pl.when(hid == 1)
    def _():
        xsend(1, 0, 1, 0, 256)
        xsend(1, 2, 1, 0, 64)
        xsend(1, 3, 1, 0, 64)
        xsend(1, 0, 1, 256, 512)

    @pl.when(hid == 3)
    def _():
        xsend(3, 0, 3, 0, 256)
        xsend(3, 2, 3, 0, 64)
        xsend(3, 1, 3, 0, 128)
        xsend(3, 0, 3, 256, 512)

    @pl.when(hid == 0)
    def _():
        xsend(0, 1, 0, 0, 128)
        xsend(0, 3, 0, 0, 64)
        xsend(0, 2, 0, 0, 64)

    def forward_tokens(part):
        @pl.when(hid == 1)
        def _():
            xrecv(2, 1, 2, 256 * part, 256 * part + 128)
            xsend(1, 0, 2, 256 * part, 256 * part + 128)

        @pl.when(hid == 3)
        def _():
            xrecv(2, 3, 2, 256 * part + 128, 256 * part + 256)
            xsend(3, 0, 2, 256 * part + 128, 256 * part + 256)

    recv(("vy", 0), vf.at[z, y3, c])
    send(("vyf", 0), vf.at[z, y3, c, :, pl.ds(0, 512)], vf.at[z, y3, c, :, pl.ds(0, 512)], yp)
    recv(("vy", 1), vf.at[z, y1, c])
    send(("vyf", 1), vf.at[z, y1, c, :, pl.ds(512, 512)], vf.at[z, y1, c, :, pl.ds(512, 512)], ym)
    for i in (1, 2):
        u_z_recv(*order[i])
        u_z(order[i][0], 1)
        u_y(i, z_of[i])
    recv(("vyf", 0), vf.at[z, y2, c, :, pl.ds(0, 512)])
    recv(("vyf", 1), vf.at[z, y2, c, :, pl.ds(512, 512)])
    for half in (0, 1):
        for direction in (0, 1):
            v_z(direction, half, 0)
    send(("vc", 0), vf.at[z, :, c], vf.at[z, :, c], mate)
    u_y_recv(0, z)
    forward_tokens(0)
    for i in (3, 4):
        u_z_recv(*order[i])
        if order[i][0] == 0 or order[i][1] < 2:
            u_z(order[i][0], 2)
        u_y(i, z_of[i])
    u_y_recv(1, z_of[1])
    u_y_recv(2, z_of[2])

    def v_hop(s):
        for half in (0, 1):
            for direction in (0, 1):
                last = 3 if half == direction else 2
                if s > last:
                    continue
                v_z_recv(direction, half, s)
                if s < last:
                    v_z(direction, half, s + 1)
        if s < 3:
            for k, zz in ((0, zmod(z - s - 1)), (1, zmod(z + s + 1))):
                send(("vc", 1 + 2 * s + k), vf.at[zz, :, c], vf.at[zz, :, c], mate)
        else:
            zz = zmod(z + 4)
            send(("vc", 7), vf.at[zz, :, c], vf.at[zz, :, c], mate)

    v_hop(0)
    forward_tokens(1)
    for i in (5, 6):
        u_z_recv(*order[i])
        if order[i][0] == 0:
            u_z(0, 3)
        u_y(i, z_of[i])
    u_y_recv(3, z_of[3])
    u_y_recv(4, z_of[4])
    u_z_recv(0, 3)
    u_y(7, z_of[7])
    v_hop(1)
    send(("uc", 0), uf.at[:, y, c], uf.at[:, y, c], mate)
    u_y_recv(5, z_of[5])
    u_y_recv(6, z_of[6])
    u_y_recv(7, z_of[7])
    send(("uc", 1), uf.at[:, y1, c], uf.at[:, y1, c], mate)
    send(("uc", 2), uf.at[:, y3, c], uf.at[:, y3, c], mate)
    v_hop(2)
    v_hop(3)
    for i in range(8):
        recv(("uyf", i), uf.at[z, y2, c])
    send(("uc", 3), uf.at[:, y2, c], uf.at[:, y2, c], mate)
    for i in range(4):
        recv(("uc", i), uf.at[:, y, 1 - c])
    for i in range(8):
        recv(("vc", i), vf.at[z, :, 1 - c])

    def units(lo_row, n_row, lo_tile, hi_tile, count):
        rows = pl.ds(lo_row, n_row)

        def body(j, carry):
            cols = pl.ds(pl.multiple_of(j * TILE, TILE), TILE)
            u = uf[:, :, :, :, cols].reshape(D, TILE)
            v = vf[:, :, :, :, cols].reshape(D, TILE)
            pre = jnp.dot(xg[0, rows, :], u, preferred_element_type=F32)
            gh = jnp.dot(xg[1, rows, :], v, preferred_element_type=F32)
            act, slope = gelu_pair(pre)
            pg = gh * slope
            if count is not None:
                row = lax.broadcasted_iota(jnp.int32, (n_row, TILE), 0).astype(F32) + lo_row
                keep = row < count
                act = jnp.where(keep, act, 0.0)
                pg = jnp.where(keep, pg, 0.0)
            hbuf[rows, cols] = act.astype(BF16)
            pbuf[rows, cols] = pg.astype(BF16)
            return carry

        lax.fori_loop(lo_tile, hi_tile, body, 0)

    def outputs(plane, d, lo_row, n_row, n_unit):
        rows = pl.ds(lo_row, n_row)
        for a, val, w in ((0, hbuf, vf), (1, pbuf, uf)):
            wt = w[2 * d:2 * d + 2].reshape(COLS, UNITS)[:, :n_unit]
            out = lax.dot_general(val[rows, :n_unit], wt, NT, preferred_element_type=F32)
            if d == plane:
                ro[plane, a, rows, :] = out.astype(BF16)
            else:
                so[d, a, rows, :] = out.astype(BF16)

    def osend(src, dst, d, lo, hi, via=False):
        part = so.at[d, :, pl.ds(lo, hi - lo), :]
        to = fo.at[:, pl.ds(lo, hi - lo), :] if via else ro.at[src, :, pl.ds(lo, hi - lo), :]
        send(("o", src, dst, d, lo), part, to, xs[(dst - src) % 4 - 1], src,
             lambda: so.at[d, :, pl.ds(lo, hi - lo), :])

    def orecv(src, lo, hi, dst):
        recv(("o", src, dst, dst, lo), ro.at[src, :, pl.ds(lo, hi - lo), :])

    def grads(full, n_row):
        for a, val in ((1, hbuf), (0, pbuf)):
            def body(dt, carry):
                cols = pl.ds(pl.multiple_of(dt * COLS, COLS), COLS)
                if full:
                    left = lax.dot_general(
                        xg[a, :, cols], val[:, :512], TN, preferred_element_type=F32)
                    right = lax.dot_general(
                        xg[a, :256, cols], val[:256, 512:], TN, preferred_element_type=F32)
                    g = jnp.concatenate([left, right], axis=1)
                else:
                    g = lax.dot_general(
                        xg[a, :n_row, cols], val[:n_row, :], TN, preferred_element_type=F32)
                g = g.reshape(2, NY, 2, 16, UNITS)
                lane[a, pl.ds(2 * dt, 2)] = jnp.where(c == 0, g[:, :, 0], g[:, :, 1])
                gsend[a, pl.ds(2 * dt, 2)] = jnp.where(c == 0, g[:, :, 1], g[:, :, 0]).astype(BF16)
                return carry

            lax.fori_loop(0, 4, body, 0)

    @pl.when(hid == 0)
    def _():
        xrecv(1, 0, 1, 0, 256)
        xrecv(3, 0, 3, 0, 256)
        xrecv(1, 0, 2, 0, 128)
        xrecv(3, 0, 2, 128, 256)
        units(0, 256, 0, 2, None)
        units(0, 256, 2, 4, wider[1])
        for d in (2, 1, 3, 0):
            outputs(0, d, 0, 256, 1024)
            if d == 2:
                osend(0, 1, 2, 0, 128, True)
                osend(0, 3, 2, 128, 256, True)
            elif d:
                osend(0, d, d, 0, 256)
        xrecv(1, 0, 1, 256, 512)
        xrecv(3, 0, 3, 256, 512)
        xrecv(1, 0, 2, 256, 384)
        xrecv(3, 0, 2, 384, 512)
        units(256, 256, 0, 2, None)
        for d in (2, 1, 3, 0):
            outputs(0, d, 256, 256, 512)
            if d == 2:
                osend(0, 1, 2, 256, 384, True)
                osend(0, 3, 2, 384, 512, True)
            elif d:
                osend(0, d, d, 256, 512)
        grads(True, 512)

    @pl.when(hid == 1)
    def _():
        xrecv(0, 1, 0, 0, 128)
        xrecv(3, 1, 3, 0, 128)
        units(0, 128, 0, 4, wider[2])
        for d in (0, 3, 2, 1):
            outputs(1, d, 0, 128, 1024)
            if d != 1:
                osend(1, d, d, 0, 128)
        grads(False, 128)

    @pl.when(hid == 2)
    def _():
        for s in (0, 1, 3):
            xrecv(s, 2, s, 0, 64)
        units(0, 64, 0, 4, wider[3])
        for d in (0, 1, 3, 2):
            outputs(2, d, 0, 64, 1024)
            if d != 2:
                osend(2, d, d, 0, 64)
        grads(False, 64)

    @pl.when(hid == 3)
    def _():
        for s in (0, 1, 2):
            xrecv(s, 3, s, 0, 64)
        units(0, 64, 0, 4, wider[3])
        for d in (1, 0, 2, 3):
            outputs(3, d, 0, 64, 1024)
            if d != 3:
                osend(3, d, d, 0, 64)
        grads(False, 64)

    for a in (1, 0):
        send(("gc", a), gsend.at[a], grecv.at[a], mate)

    def forward_outputs(part):
        for plane, lo in ((1, 256 * part), (3, 256 * part + 128)):
            @pl.when(hid == plane)
            def _():
                recv(("o", 0, plane, 2, lo), fo.at[:, pl.ds(lo, 128), :])
                send(("of", plane, lo), fo.at[:, pl.ds(lo, 128), :],
                     ro.at[0, :, pl.ds(lo, 128), :], xs[(2 - plane) % 4 - 1], plane,
                     lambda lo=lo: fo.at[:, pl.ds(lo, 128), :])

    def total(a, zz, yy):
        return lane[a, zz, yy] + grecv[a, zz, yy].astype(F32)

    def v_step(direction, s):
        zz = zmod(z + 4 - s) if direction == 0 else zmod(z - 4 + s)
        first, last = 2 * direction, 2 * direction + 2
        for yy in range(NY):
            if s == 0 and not first <= yy < last:
                continue
            val = total(1, zz, yy)
            if s > 1 or (s == 1 and first <= yy < last):
                val = val + rv[direction, s - 1, yy].astype(F32)
            sv[direction, s, yy] = val.astype(BF16)
        ys = pl.ds(first, 2) if s == 0 else pl.ds(0, NY)
        send(("v", direction, s), sv.at[direction, s, ys], rv.at[direction, s, ys],
             zp if direction == 0 else zm)

    def v_step_recv(direction, s):
        ys = pl.ds(2 * direction, 2) if s == 0 else pl.ds(0, NY)
        recv(("v", direction, s), rv.at[direction, s, ys])

    recv(("gc", 1), grecv.at[1])
    v_step(0, 0)
    v_step(1, 0)
    recv(("gc", 0), grecv.at[0])
    for k, dev in ((0, yp), (1, ym)):
        for i in range(4):
            su0[k, i] = total(0, 4 * k + i, y2).astype(BF16)
        send(("u0", k), su0.at[k], ru0.at[k], dev)
    forward_outputs(0)
    for direction in (0, 1):
        v_step_recv(direction, 0)
        v_step(direction, 1)
    for k, dev, yy in ((0, yp, y1), (1, ym, y3)):
        recv(("u0", k), ru0.at[k])
        for i in range(NZ):
            val = total(0, i, yy)
            if i // 4 == k:
                val = val + ru0[k, i % 4].astype(F32)
            su1[k, i] = val.astype(BF16)
        send(("u1", k), su1.at[k], ru1.at[k], dev)
    for s in (1, 2):
        for direction in (0, 1):
            v_step_recv(direction, s)
            v_step(direction, s + 1)
    forward_outputs(1)
    recv(("u1", 0), ru1.at[0])
    recv(("u1", 1), ru1.at[1])
    for i in range(NZ):
        uy[i] = total(0, i, y) + ru1[0, i].astype(F32) + ru1[1, i].astype(F32)

    def u_step(direction, s):
        zz = zmod(z + 4 - s) if direction == 0 else zmod(z - 3 + s)
        val = uy[zz]
        if s:
            val = val + ruz[direction, s - 1].astype(F32)
        suz[direction, s] = val.astype(BF16)
        send(("u", direction, s), suz.at[direction, s], ruz.at[direction, s],
             zp if direction == 0 else zm)

    def u_step_recv(direction, s):
        recv(("u", direction, s), ruz.at[direction, s])

    u_step(0, 0)
    u_step(1, 0)
    v_step_recv(0, 3)
    v_step_recv(1, 3)
    for yy in range(NY):
        vz[yy] = total(1, z, yy) + rv[0, 3, yy].astype(F32) + rv[1, 3, yy].astype(F32)
    for k, dev in ((0, yp), (1, ym)):
        svy0[k] = vz[y2, :, 512 * k:512 * k + 512].astype(BF16)
        send(("vy0", k), svy0.at[k], rvy0.at[k], dev)
    u_step_recv(0, 0)
    u_step(0, 1)
    u_step_recv(1, 0)
    u_step(1, 1)
    for k, dev, yy in ((0, yp, y1), (1, ym, y3)):
        recv(("vy0", k), rvy0.at[k])
        own = vz[yy]
        got = rvy0[k].astype(F32)
        if k == 0:
            val = jnp.concatenate([own[:, :512] + got, own[:, 512:]], axis=1)
        else:
            val = jnp.concatenate([own[:, :512], own[:, 512:] + got], axis=1)
        svy1[k] = val.astype(BF16)
        send(("vy1", k), svy1.at[k], rvy1.at[k], dev)
    u_step_recv(0, 1)
    u_step(0, 2)
    u_step_recv(1, 1)
    u_step(1, 2)
    u_step_recv(0, 2)
    u_step(0, 3)
    for k in (0, 1):
        recv(("vy1", k), rvy1.at[k])
    gdown_ref[...] = vz[y] + rvy1[0].astype(F32) + rvy1[1].astype(F32)

    @pl.when(hid == 0)
    def _():
        orecv(1, 0, 128, 0)
        orecv(2, 0, 64, 0)
        orecv(3, 0, 64, 0)

    for plane in (1, 3):
        @pl.when(hid == plane)
        def _():
            orecv(0, 0, 256, plane)
            orecv(0, 256, 512, plane)
            for s, n in ((1, 128), (2, 64), (3, 64)):
                if s != plane:
                    orecv(s, 0, n, plane)

    @pl.when(hid == 2)
    def _():
        for plane, lo in ((1, 0), (3, 128), (1, 256), (3, 384)):
            recv(("of", plane, lo), ro.at[0, :, pl.ds(lo, 128), :])
        orecv(1, 0, 128, 2)
        orecv(3, 0, 64, 2)

    for a, ref in ((0, mixed_ref), (1, gtok_ref)):
        top = ro[0, a, 0:128].astype(F32) + ro[1, a, 0:128].astype(F32)
        wide = top[:64] + ro[2, a, 0:64].astype(F32) + ro[3, a, 0:64].astype(F32)
        ro[0, a, 0:128] = jnp.concatenate([wide, top[64:]], axis=0).astype(BF16)
        ref[...] = jnp.dot(permt[...], ro[0, a], preferred_element_type=F32).astype(BF16)

    u_step_recv(1, 2)
    u_step_recv(0, 3)
    gup_ref[...] = uy[z] + ruz[0, 3].astype(F32) + ruz[1, 2].astype(F32)

    def left(which):
        for key, src, plane in sent:
            if plane == which:
                msg(key, src(), src(), mate).wait_send()

    left(None)
    for plane in range(4):
        @pl.when(hid == plane)
        def _():
            left(plane)
    assert len(slots) <= N_SEM, len(slots)


def per_device(tokens, width_index, up_weight, down_weight, cotangent):
    vm = pl.BlockSpec(memory_space=pltpu.VMEM)
    block = (16, UNITS)

    def buf(*shape):
        return pltpu.VMEM(shape, BF16)

    mixed, gtok, gup, gdown = pl.pallas_call(
        kernel,
        out_shape=(
            jax.ShapeDtypeStruct((ROWS, COLS), BF16),
            jax.ShapeDtypeStruct((ROWS, COLS), BF16),
            jax.ShapeDtypeStruct(block, F32),
            jax.ShapeDtypeStruct(block, F32),
        ),
        in_specs=[vm] * 5,
        out_specs=(vm,) * 4,
        scratch_shapes=[
            buf(NZ, NY, 2, *block), buf(NZ, NY, 2, *block),
            buf(2, ROWS, D), buf(ROWS, UNITS), buf(ROWS, UNITS),
            buf(4, 2, ROWS, COLS), buf(4, 2, ROWS, COLS), buf(2, ROWS, COLS),
            buf(ROWS, ROWS), buf(ROWS, ROWS),
            buf(2, NZ, NY, *block), buf(2, NZ, NY, *block),
            pltpu.VMEM((2, NZ, NY, *block), F32),
            buf(2, 4, NY, *block), buf(2, 4, NY, *block),
            buf(2, 4, *block), buf(2, 4, *block),
            buf(2, NZ, *block), buf(2, NZ, *block),
            buf(2, 4, *block), buf(2, 4, *block),
            buf(2, 16, 512), buf(2, 16, 512),
            buf(2, *block), buf(2, *block),
            pltpu.VMEM((NZ, *block), F32), pltpu.VMEM((NY, *block), F32),
            pltpu.SemaphoreType.DMA((N_SEM,)), pltpu.SemaphoreType.DMA((N_SEM,)),
        ],
        compiler_params=pltpu.CompilerParams(
            collective_id=0, has_side_effects=True, vmem_limit_bytes=56 * 1024 * 1024,
        ),
    )(tokens, width_index.reshape(1, ROWS), up_weight, down_weight.T, cotangent)
    return mixed, gtok, gup, gdown.T


def solution(mesh):
    placed = (P("tok", "hid"), P("tok"), P("tok", "hid"), P("hid", "tok"), P("tok", "hid"))
    return jax.shard_map(
        per_device,
        mesh=mesh,
        in_specs=placed,
        out_specs=(P("tok", "hid"), P("tok", "hid"), P("tok", "hid"), P("hid", "tok")),
        check_vma=False,
    )
```

time: 616 us -> 85.7 us (0.14)
  the two profiles are of different devices: /device:TPU:1 before, /device:TPU:32 now
where the time goes in v1:
time: 85.7 us; the launch traced here: 85.5 us
  Pallas kernels  80.8 us (94%)
  local copies, waits for them, and re-layouts  4.07 us (5%)
    pallas_call x1, Pallas kernels, per_device(): pl.pallas_call(kernel, out_shape=(jax.ShapeDtypeStruct((ROWS, COLS), BF16...  80.8 us
    unnamed x10, local copies, waits for them, and re-layouts  4.07 us

profile of v1, /device:TPU:32, one launch (start us, length us, event | category | flops | bytes accessed | tf_op | source)
XLA Modules:
  0.0 85.5 jit_solution(1415565610115969556)
XLA Ops:
  0.6 80.8 %shard_map.84 = (bf16[512,256]{1,0:T(8,128)(2,1)}, bf16[512,256]{1,0:T(8,128)(2,1)}, f32[16,1024]{1,0:T(8,128)}, f32[16,1024]{1,0:T(8,128)}) custom-call(bf16[512,256]{1,0:T(8,128)(2,1)} %tok_ref.1, s32[1,512]{1,0:T(1,128)} %bitcast.5, bf16[16,1024]{1,0:T(8,128)(2,1)} %up_ref.1, bf16[16,1024]{1,0:T(8,128)(2,1)} %bitcast.4, bf16[512,256]{1,0:T(8,128)(2,1)} %cot_ref.1), custom_call_target="tpu_custom_call" | custom-call | tf_op jit(solution)/shard_map/pallas_call | solution.py:553
  81.4 0.0 copy-start
  81.4 1.7 %copy.13 = bf16[512,256]{1,0:T(8,128)(2,1)} copy(bf16[512,256]{1,0:T(8,128)(2,1)} %get-tuple-element.16) | data formatting | bytes 524288
  83.1 0.0 copy-done
  83.1 0.0 copy-start.2
  83.2 0.7 copy.14
  83.9 0.2 copy-done.2
  84.0 0.0 copy-start.1
  84.0 0.6 copy.15
  84.6 0.2 copy-done.1
  84.9 0.6 copy.16
Async XLA Ops:
  81.4 1.7 %copy-start = (bf16[512,256]{1,0:T(8,128)(2,1)S(1)}, bf16[512,256]{1,0:T(8,128)(2,1)}, u32[]{:S(2)}) copy-start(bf16[512,256]{1,0:T(8,128)(2,1)} %get-tuple-element.17) | copy-start | bytes 786436
  83.1 0.9 %copy-start.2 = (f32[16,1024]{1,0:T(8,128)S(1)}, f32[16,1024]{1,0:T(8,128)}, u32[]{:S(2)}) copy-start(f32[16,1024]{1,0:T(8,128)} %get-tuple-element.18) | copy-start | bytes 196612
  84.0 0.9 %copy-start.1 = (f32[16,1024]{1,0:T(8,128)S(1)}, f32[16,1024]{1,0:T(8,128)}, u32[]{:S(2)}) copy-start(f32[16,1024]{1,0:T(8,128)} %get-tuple-element.11) | copy-start | bytes 196612

commit v2 on v1

--- a/solution.py
+++ b/solution.py
@@ -17,7 +17,7 @@
 UNITS = 1024
 NZ, NY = 8, 4
 TILE = 256
-N_SEM = 128
+N_SEM = 224
 
 NT = (((1,), (1,)), ((), ()))
 TN = (((0,), (0,)), ((), ()))
@@ -33,7 +33,7 @@
     mixed_ref, gtok_ref, gup_ref, gdown_ref,
     uf, vf, xg, hbuf, pbuf, so, ro, fo, perm, permt,
     gsend, grecv, lane,
-    sv, rv, su0, ru0, su1, ru1, suz, ruz, svy0, rvy0, svy1, rvy1, uy, vz,
+    sv, rv, su1, ru1, suz, ruz, svy, rvy, uy, vz,
     ssem, rsem,
 ):
     hid = lax.axis_index("hid")
@@ -52,9 +52,9 @@
         return {"tok": (zz * NY + yy) * 2 + cc}
 
     zp, zm = at(zmod(z + 1), y, c), at(zmod(z - 1), y, c)
-    yp, ym = at(z, ymod(y + 1), c), at(z, ymod(y - 1), c)
     mate = at(z, y, 1 - c)
-    near = (zp, zm, yp, ym, mate)
+    near = [at(zmod(z + k), y, c) for k in (1, -1, 2, -2, 3, -3, 4)]
+    near += [at(z, ymod(y + r), c) for r in (1, 2, 3)] + [mate]
     xs = [{"hid": lax.rem(hid + k, 4)} for k in (1, 2, 3)]
 
     slots = {}
@@ -77,7 +77,7 @@
         msg(key, dst, dst, mate).wait_recv()
 
     barrier = pltpu.get_barrier_semaphore()
-    for dev in near + tuple(xs):
+    for dev in near + xs:
         pl.semaphore_signal(barrier, inc=1, device_id=dev, device_id_type=MESH)
 
     uf[z, y, c] = up_ref[...]
@@ -85,43 +85,61 @@
 
     pl.semaphore_wait(barrier, len(near) + len(xs))
 
-    y1, y3, y2 = ymod(y + 1), ymod(y - 1), ymod(y + 2)
-
-    def u_z(direction, s):
-        zz = zmod(z - s) if direction == 0 else zmod(z + s)
-        send(("uz", direction, s), uf.at[zz, y, c], uf.at[zz, y, c], zp if direction == 0 else zm)
-
-    def u_z_recv(direction, s):
-        recv(("uz", direction, s), uf.at[z, y, c])
-
-    def u_y(i, zz):
-        for k, dev in ((0, yp), (1, ym)):
-            send(("uy", i, k), uf.at[zz, y, c], uf.at[zz, y, c], dev)
-
-    def u_y_recv(i, zz):
-        recv(("uy", i, 0), uf.at[zz, y3, c])
-        recv(("uy", i, 1), uf.at[zz, y1, c])
-        if i % 2 == 0:
-            send(("uyf", i), uf.at[zz, y3, c], uf.at[zz, y3, c], yp)
-        else:
-            send(("uyf", i), uf.at[zz, y1, c], uf.at[zz, y1, c], ym)
-
-    def v_z(direction, half, s):
-        zz = zmod(z - s) if direction == 0 else zmod(z + s)
-        ref = vf.at[zz, pl.ds(2 * half, 2), c]
-        send(("vz", direction, half, s), ref, ref, zp if direction == 0 else zm)
-
-    def v_z_recv(direction, half, s):
-        recv(("vz", direction, half, s), vf.at[z, pl.ds(2 * half, 2), c])
-
-    order = [(None, 0), (0, 0), (1, 0), (0, 1), (1, 1), (0, 2), (1, 2), (0, 3)]
-    z_of = [z] + [zmod(z - s - 1) if d == 0 else zmod(z + s + 1) for d, s in order[1:]]
-
-    send(("vy", 0), vf.at[z, y, c], vf.at[z, y, c], yp)
-    send(("vy", 1), vf.at[z, y, c], vf.at[z, y, c], ym)
-    u_z(0, 0)
-    u_z(1, 0)
-    u_y(0, z)
+    def peer_y(r):
+        return ymod(y + r)
+
+    def u_share(k):
+        zz = zmod(z + k)
+        for r in (1, 3, 2):
+            ref = uf.at[zz, y, c]
+            send(("uy", k, r), ref, ref, at(z, peer_y(r), c))
+
+    def u_direct(k):
+        ref = uf.at[z, y, c]
+        send(("uz", k), ref, ref, at(zmod(z + k), y, c))
+
+    def u_pass(k, step):
+        ref = uf.at[zmod(z + k), y, c]
+        send(("uz", step - k), ref, ref, at(zmod(z + step), y, c))
+
+    def u_recv(k):
+        recv(("uz", -k if k != 4 else 4), uf.at[z, y, c])
+
+    def u_group(k):
+        for r in (1, 3, 2):
+            recv(("uy", k, r), uf.at[z, y, c])
+        zz = zmod(z + k)
+        send(("uc", k), uf.at[zz, :, c], uf.at[zz, :, c], mate)
+
+    def hops(r, d):
+        return 4 if (r < 2) == (d == 0) else 3
+
+    def v_send(r, d, s):
+        zz = zmod(z - s) if d == 0 else zmod(z + s)
+        ref = vf.at[zz, peer_y(r), c]
+        send(("vz", r, d, s), ref, ref, zp if d == 0 else zm)
+
+    def v_recv(r, d, s):
+        if s < hops(r, d):
+            recv(("vz", r, d, s), vf.at[z, y, c])
+            if s + 1 < hops(r, d):
+                v_send(r, d, s + 1)
+
+    def v_mate(k):
+        zz = zmod(z + k)
+        send(("vc", k), vf.at[zz, :, c], vf.at[zz, :, c], mate)
+
+    own_v = vf.at[z, y, c]
+    for r in (1, 3, 2):
+        send(("vy", r), own_v, own_v, at(z, peer_y(r), c))
+    v_send(0, 0, 0)
+    v_send(0, 1, 0)
+    u_direct(1)
+    u_direct(-1)
+    u_share(0)
+    u_direct(2)
+    u_direct(-2)
+    u_direct(4)
 
     wid = wid_ref[...]
     level = lax.broadcasted_iota(jnp.int32, (8, ROWS), 0)
@@ -199,73 +217,57 @@
             xrecv(2, 3, 2, 256 * part + 128, 256 * part + 256)
             xsend(3, 0, 2, 256 * part + 128, 256 * part + 256)
 
-    recv(("vy", 0), vf.at[z, y3, c])
-    send(("vyf", 0), vf.at[z, y3, c, :, pl.ds(0, 512)], vf.at[z, y3, c, :, pl.ds(0, 512)], yp)
-    recv(("vy", 1), vf.at[z, y1, c])
-    send(("vyf", 1), vf.at[z, y1, c, :, pl.ds(512, 512)], vf.at[z, y1, c, :, pl.ds(512, 512)], ym)
-    for i in (1, 2):
-        u_z_recv(*order[i])
-        u_z(order[i][0], 1)
-        u_y(i, z_of[i])
-    recv(("vyf", 0), vf.at[z, y2, c, :, pl.ds(0, 512)])
-    recv(("vyf", 1), vf.at[z, y2, c, :, pl.ds(512, 512)])
-    for half in (0, 1):
-        for direction in (0, 1):
-            v_z(direction, half, 0)
-    send(("vc", 0), vf.at[z, :, c], vf.at[z, :, c], mate)
-    u_y_recv(0, z)
+    for r in (3, 1, 2):
+        recv(("vy", (4 - r) % 4), own_v)
+        v_send(r, 0, 0)
+        v_send(r, 1, 0)
+    for k in (1, -1):
+        u_recv(k)
+        u_share(k)
+    v_recv(0, 0, 0)
+    v_recv(0, 1, 0)
+    for k in (2, -2):
+        u_recv(k)
+        u_pass(k, -1 if k > 0 else 1)
+        u_share(k)
+    u_recv(4)
+    u_share(4)
     forward_tokens(0)
-    for i in (3, 4):
-        u_z_recv(*order[i])
-        if order[i][0] == 0 or order[i][1] < 2:
-            u_z(order[i][0], 2)
-        u_y(i, z_of[i])
-    u_y_recv(1, z_of[1])
-    u_y_recv(2, z_of[2])
-
-    def v_hop(s):
-        for half in (0, 1):
-            for direction in (0, 1):
-                last = 3 if half == direction else 2
-                if s > last:
-                    continue
-                v_z_recv(direction, half, s)
-                if s < last:
-                    v_z(direction, half, s + 1)
-        if s < 3:
-            for k, zz in ((0, zmod(z - s - 1)), (1, zmod(z + s + 1))):
-                send(("vc", 1 + 2 * s + k), vf.at[zz, :, c], vf.at[zz, :, c], mate)
-        else:
-            zz = zmod(z + 4)
-            send(("vc", 7), vf.at[zz, :, c], vf.at[zz, :, c], mate)
-
-    v_hop(0)
+    for r in (3, 1, 2):
+        v_recv(r, 0, 0)
+        v_recv(r, 1, 0)
+    v_mate(0)
+    v_mate(-1)
+    v_mate(1)
+    for k in (3, -3):
+        u_recv(k)
+        u_share(k)
+    u_group(0)
+    for r in range(4):
+        v_recv(r, 0, 1)
+        v_recv(r, 1, 1)
+    v_mate(-2)
+    v_mate(2)
+    u_group(1)
+    u_group(-1)
     forward_tokens(1)
-    for i in (5, 6):
-        u_z_recv(*order[i])
-        if order[i][0] == 0:
-            u_z(0, 3)
-        u_y(i, z_of[i])
-    u_y_recv(3, z_of[3])
-    u_y_recv(4, z_of[4])
-    u_z_recv(0, 3)
-    u_y(7, z_of[7])
-    v_hop(1)
-    send(("uc", 0), uf.at[:, y, c], uf.at[:, y, c], mate)
-    u_y_recv(5, z_of[5])
-    u_y_recv(6, z_of[6])
-    u_y_recv(7, z_of[7])
-    send(("uc", 1), uf.at[:, y1, c], uf.at[:, y1, c], mate)
-    send(("uc", 2), uf.at[:, y3, c], uf.at[:, y3, c], mate)
-    v_hop(2)
-    v_hop(3)
-    for i in range(8):
-        recv(("uyf", i), uf.at[z, y2, c])
-    send(("uc", 3), uf.at[:, y2, c], uf.at[:, y2, c], mate)
-    for i in range(4):
-        recv(("uc", i), uf.at[:, y, 1 - c])
-    for i in range(8):
-        recv(("vc", i), vf.at[z, :, 1 - c])
+    for r in range(4):
+        v_recv(r, 0, 2)
+        v_recv(r, 1, 2)
+    v_mate(-3)
+    v_mate(3)
+    u_group(2)
+    u_group(-2)
+    u_group(4)
+    for r in range(4):
+        v_recv(r, 0, 3)
+        v_recv(r, 1, 3)
+    v_mate(4)
+    u_group(3)
+    u_group(-3)
+    for k in (0, -1, 1, -2, 2, -3, 3, 4):
+        recv(("uc", k), uf.at[z, :, 1 - c])
+        recv(("vc", k), vf.at[z, :, 1 - c])
 
     def units(lo_row, n_row, lo_tile, hi_tile, count):
         rows = pl.ds(lo_row, n_row)
@@ -308,11 +310,16 @@
     def orecv(src, lo, hi, dst):
         recv(("o", src, dst, dst, lo), ro.at[src, :, pl.ds(lo, hi - lo), :])
 
-    def grads(full, n_row):
-        for a, val in ((1, hbuf), (0, pbuf)):
-            def body(dt, carry):
-                cols = pl.ds(pl.multiple_of(dt * COLS, COLS), COLS)
-                if full:
+    def tile(i):
+        return lax.rem(lax.div(z, 2) + (2, 1, 3, 0)[i], 4)
+
+    def grads(plane, n_row):
+        for i in range(4):
+            dt = tile(i)
+            cols = pl.ds(pl.multiple_of(dt * COLS, COLS), COLS)
+            zs = pl.ds(2 * dt, 2)
+            for a, val in ((1, hbuf), (0, pbuf)):
+                if plane == 0:
                     left = lax.dot_general(
                         xg[a, :, cols], val[:, :512], TN, preferred_element_type=F32)
                     right = lax.dot_general(
@@ -322,11 +329,14 @@
                     g = lax.dot_general(
                         xg[a, :n_row, cols], val[:n_row, :], TN, preferred_element_type=F32)
                 g = g.reshape(2, NY, 2, 16, UNITS)
-                lane[a, pl.ds(2 * dt, 2)] = jnp.where(c == 0, g[:, :, 0], g[:, :, 1])
-                gsend[a, pl.ds(2 * dt, 2)] = jnp.where(c == 0, g[:, :, 1], g[:, :, 0]).astype(BF16)
-                return carry
-
-            lax.fori_loop(0, 4, body, 0)
+                lane[a, zs] = jnp.where(c == 0, g[:, :, 0], g[:, :, 1])
+                gsend[a, zs] = jnp.where(c == 0, g[:, :, 1], g[:, :, 0]).astype(BF16)
+                send(("gc", a, i), gsend.at[a, zs], grecv.at[a, zs], mate, plane,
+                     lambda: gsend.at[0, pl.ds(0, 2)])
+
+    def mate_grads(a, tiles):
+        for i in tiles:
+            recv(("gc", a, i), grecv.at[a, pl.ds(0, 2)])
 
     @pl.when(hid == 0)
     def _():
@@ -355,7 +365,7 @@
                 osend(0, 3, 2, 384, 512, True)
             elif d:
                 osend(0, d, d, 256, 512)
-        grads(True, 512)
+        grads(0, 512)
 
     @pl.when(hid == 1)
     def _():
@@ -366,7 +376,7 @@
             outputs(1, d, 0, 128, 1024)
             if d != 1:
                 osend(1, d, d, 0, 128)
-        grads(False, 128)
+        grads(1, 128)
 
     @pl.when(hid == 2)
     def _():
@@ -377,7 +387,7 @@
             outputs(2, d, 0, 64, 1024)
             if d != 2:
                 osend(2, d, d, 0, 64)
-        grads(False, 64)
+        grads(2, 64)
 
     @pl.when(hid == 3)
     def _():
@@ -388,10 +398,7 @@
             outputs(3, d, 0, 64, 1024)
             if d != 3:
                 osend(3, d, d, 0, 64)
-        grads(False, 64)
-
-    for a in (1, 0):
-        send(("gc", a), gsend.at[a], grecv.at[a], mate)
+        grads(3, 64)
 
     def forward_outputs(part):
         for plane, lo in ((1, 256 * part), (3, 256 * part + 128)):
@@ -405,98 +412,73 @@
     def total(a, zz, yy):
         return lane[a, zz, yy] + grecv[a, zz, yy].astype(F32)
 
-    def v_step(direction, s):
-        zz = zmod(z + 4 - s) if direction == 0 else zmod(z - 4 + s)
-        first, last = 2 * direction, 2 * direction + 2
-        for yy in range(NY):
-            if s == 0 and not first <= yy < last:
-                continue
-            val = total(1, zz, yy)
-            if s > 1 or (s == 1 and first <= yy < last):
-                val = val + rv[direction, s - 1, yy].astype(F32)
-            sv[direction, s, yy] = val.astype(BF16)
-        ys = pl.ds(first, 2) if s == 0 else pl.ds(0, NY)
-        send(("v", direction, s), sv.at[direction, s, ys], rv.at[direction, s, ys],
-             zp if direction == 0 else zm)
-
-    def v_step_recv(direction, s):
-        ys = pl.ds(2 * direction, 2) if s == 0 else pl.ds(0, NY)
-        recv(("v", direction, s), rv.at[direction, s, ys])
-
-    recv(("gc", 1), grecv.at[1])
-    v_step(0, 0)
-    v_step(1, 0)
-    recv(("gc", 0), grecv.at[0])
-    for k, dev in ((0, yp), (1, ym)):
-        for i in range(4):
-            su0[k, i] = total(0, 4 * k + i, y2).astype(BF16)
-        send(("u0", k), su0.at[k], ru0.at[k], dev)
+    def ring_send(r, d, s):
+        zz = zmod(z + 4 - s) if d == 0 else zmod(z - 4 + s)
+        val = total(1, zz, peer_y(r))
+        if s > 4 - hops(r, d):
+            val = val + rv[d, s - 1, r].astype(F32)
+        sv[d, s, r] = val.astype(BF16)
+        send(("v", r, d, s), sv.at[d, s, r], rv.at[d, s, r], zp if d == 0 else zm)
+
+    def ring_step(s):
+        for r in range(4):
+            for d in (0, 1):
+                if s > 4 - hops(r, d):
+                    recv(("v", r, d, s - 1), rv.at[d, s - 1, r])
+                if s >= 4 - hops(r, d):
+                    ring_send(r, d, s)
+
+    def up_share(k):
+        for r in (1, 3, 2):
+            su1[k + 3, r] = total(0, zmod(z + k), peer_y(r)).astype(BF16)
+            send(("uu", k, r), su1.at[k + 3, r], ru1.at[k + 3, r], at(z, peer_y(r), c))
+
+    def up_sum(k):
+        val = total(0, zmod(z + k), y)
+        for r in (1, 3, 2):
+            recv(("uu", k, r), ru1.at[k + 3, r])
+            val = val + ru1[k + 3, r].astype(F32)
+        return val
+
+    def up_direct(k):
+        suz[k + 3] = up_sum(k).astype(BF16)
+        send(("uw", k), suz.at[k + 3], ruz.at[k + 3], at(zmod(z + k), y, c))
+
+    mate_grads(1, (0,))
+    ring_step(0)
+    mate_grads(0, (0,))
+    up_share(4)
+    mate_grads(1, (1, 2))
+    ring_step(1)
+    mate_grads(0, (1, 2))
+    for k in (3, -3, 2, -2):
+        up_share(k)
     forward_outputs(0)
-    for direction in (0, 1):
-        v_step_recv(direction, 0)
-        v_step(direction, 1)
-    for k, dev, yy in ((0, yp, y1), (1, ym, y3)):
-        recv(("u0", k), ru0.at[k])
-        for i in range(NZ):
-            val = total(0, i, yy)
-            if i // 4 == k:
-                val = val + ru0[k, i % 4].astype(F32)
-            su1[k, i] = val.astype(BF16)
-        send(("u1", k), su1.at[k], ru1.at[k], dev)
-    for s in (1, 2):
-        for direction in (0, 1):
-            v_step_recv(direction, s)
-            v_step(direction, s + 1)
+    mate_grads(1, (3,))
+    ring_step(2)
+    mate_grads(0, (3,))
+    for k in (1, -1, 0):
+        up_share(k)
+    up_direct(4)
+    up_direct(3)
+    up_direct(-3)
+    ring_step(3)
     forward_outputs(1)
-    recv(("u1", 0), ru1.at[0])
-    recv(("u1", 1), ru1.at[1])
-    for i in range(NZ):
-        uy[i] = total(0, i, y) + ru1[0, i].astype(F32) + ru1[1, i].astype(F32)
-
-    def u_step(direction, s):
-        zz = zmod(z + 4 - s) if direction == 0 else zmod(z - 3 + s)
-        val = uy[zz]
-        if s:
-            val = val + ruz[direction, s - 1].astype(F32)
-        suz[direction, s] = val.astype(BF16)
-        send(("u", direction, s), suz.at[direction, s], ruz.at[direction, s],
-             zp if direction == 0 else zm)
-
-    def u_step_recv(direction, s):
-        recv(("u", direction, s), ruz.at[direction, s])
-
-    u_step(0, 0)
-    u_step(1, 0)
-    v_step_recv(0, 3)
-    v_step_recv(1, 3)
-    for yy in range(NY):
-        vz[yy] = total(1, z, yy) + rv[0, 3, yy].astype(F32) + rv[1, 3, yy].astype(F32)
-    for k, dev in ((0, yp), (1, ym)):
-        svy0[k] = vz[y2, :, 512 * k:512 * k + 512].astype(BF16)
-        send(("vy0", k), svy0.at[k], rvy0.at[k], dev)
-    u_step_recv(0, 0)
-    u_step(0, 1)
-    u_step_recv(1, 0)
-    u_step(1, 1)
-    for k, dev, yy in ((0, yp, y1), (1, ym, y3)):
-        recv(("vy0", k), rvy0.at[k])
-        own = vz[yy]
-        got = rvy0[k].astype(F32)
-        if k == 0:
-            val = jnp.concatenate([own[:, :512] + got, own[:, 512:]], axis=1)
+    up_direct(2)
+    up_direct(-2)
+    up_direct(1)
+    up_direct(-1)
+    uy[...] = up_sum(0)
+    for r in (1, 3, 2, 0):
+        val = total(1, z, peer_y(r))
+        for d in (0, 1):
+            recv(("v", r, d, 3), rv.at[d, 3, r])
+            val = val + rv[d, 3, r].astype(F32)
+        if r:
+            svy[r] = val.astype(BF16)
+            send(("vw", r), svy.at[r], rvy.at[r], at(z, peer_y(r), c))
         else:
-            val = jnp.concatenate([own[:, :512], own[:, 512:] + got], axis=1)
-        svy1[k] = val.astype(BF16)
-        send(("vy1", k), svy1.at[k], rvy1.at[k], dev)
-    u_step_recv(0, 1)
-    u_step(0, 2)
-    u_step_recv(1, 1)
-    u_step(1, 2)
-    u_step_recv(0, 2)
-    u_step(0, 3)
-    for k in (0, 1):
-        recv(("vy1", k), rvy1.at[k])
-    gdown_ref[...] = vz[y] + rvy1[0].astype(F32) + rvy1[1].astype(F32)
+            vz[...] = val
 
     @pl.when(hid == 0)
     def _():
@@ -526,9 +508,16 @@
         ro[0, a, 0:128] = jnp.concatenate([wide, top[64:]], axis=0).astype(BF16)
         ref[...] = jnp.dot(permt[...], ro[0, a], preferred_element_type=F32).astype(BF16)
 
-    u_step_recv(1, 2)
-    u_step_recv(0, 3)
-    gup_ref[...] = uy[z] + ruz[0, 3].astype(F32) + ruz[1, 2].astype(F32)
+    val = vz[...]
+    for r in (1, 3, 2):
+        recv(("vw", r), rvy.at[r])
+        val = val + rvy[r].astype(F32)
+    gdown_ref[...] = val
+    val = uy[...]
+    for k in (4, 3, -3, 2, -2, 1, -1):
+        recv(("uw", k), ruz.at[k + 3])
+        val = val + ruz[k + 3].astype(F32)
+    gup_ref[...] = val
 
     def left(which):
         for key, src, plane in sent:
@@ -568,12 +557,10 @@
             buf(2, NZ, NY, *block), buf(2, NZ, NY, *block),
             pltpu.VMEM((2, NZ, NY, *block), F32),
             buf(2, 4, NY, *block), buf(2, 4, NY, *block),
-            buf(2, 4, *block), buf(2, 4, *block),
-            buf(2, NZ, *block), buf(2, NZ, *block),
-            buf(2, 4, *block), buf(2, 4, *block),
-            buf(2, 16, 512), buf(2, 16, 512),
-            buf(2, *block), buf(2, *block),
-            pltpu.VMEM((NZ, *block), F32), pltpu.VMEM((NY, *block), F32),
+            buf(NZ, NY, *block), buf(NZ, NY, *block),
+            buf(NZ, *block), buf(NZ, *block),
+            buf(NY, *block), buf(NY, *block),
+            pltpu.VMEM(block, F32), pltpu.VMEM(block, F32),
             pltpu.SemaphoreType.DMA((N_SEM,)), pltpu.SemaphoreType.DMA((N_SEM,)),
         ],
         compiler_params=pltpu.CompilerParams(

time: 85.7 us -> 73.1 us (0.85)
  the two profiles are of different devices: /device:TPU:32 before, /device:TPU:1 now
where the time goes in v2:
time: 73.1 us; the launch traced here: 72.8 us
  Pallas kernels  68.1 us (93%)
  local copies, waits for them, and re-layouts  4.07 us (6%)
    pallas_call x1, Pallas kernels, per_device(): pl.pallas_call(kernel, out_shape=(jax.ShapeDtypeStruct((ROWS, COLS), BF16...  68.1 us
    unnamed x10, local copies, waits for them, and re-layouts  4.07 us

profile of v2, /device:TPU:1, one launch (start us, length us, event | category | flops | bytes accessed | tf_op | source)
XLA Modules:
  0.0 72.8 jit_solution(16481305941992141227)
XLA Ops:
  0.6 68.1 %shard_map.84 = (bf16[512,256]{1,0:T(8,128)(2,1)}, bf16[512,256]{1,0:T(8,128)(2,1)}, f32[16,1024]{1,0:T(8,128)}, f32[16,1024]{1,0:T(8,128)}) custom-call(bf16[512,256]{1,0:T(8,128)(2,1)} %tok_ref.1, s32[1,512]{1,0:T(1,128)} %bitcast.5, bf16[16,1024]{1,0:T(8,128)(2,1)} %up_ref.1, bf16[16,1024]{1,0:T(8,128)(2,1)} %bitcast.4, bf16[512,256]{1,0:T(8,128)(2,1)} %cot_ref.1), custom_call_target="tpu_custom_call" | custom-call | tf_op jit(solution)/shard_map/pallas_call | solution.py:542
  68.8 0.0 copy-start
  68.8 1.7 %copy.13 = bf16[512,256]{1,0:T(8,128)(2,1)} copy(bf16[512,256]{1,0:T(8,128)(2,1)} %get-tuple-element.16) | data formatting | bytes 524288
  70.5 0.0 copy-done
  70.5 0.0 copy-start.2
  70.5 0.7 copy.14
  71.2 0.2 copy-done.2
  71.3 0.0 copy-start.1
  71.3 0.6 copy.15
  72.0 0.2 copy-done.1
  72.2 0.6 copy.16
Async XLA Ops:
  68.8 1.7 %copy-start = (bf16[512,256]{1,0:T(8,128)(2,1)S(1)}, bf16[512,256]{1,0:T(8,128)(2,1)}, u32[]{:S(2)}) copy-start(bf16[512,256]{1,0:T(8,128)(2,1)} %get-tuple-element.17) | copy-start | bytes 786436
  70.5 0.9 %copy-start.2 = (f32[16,1024]{1,0:T(8,128)S(1)}, f32[16,1024]{1,0:T(8,128)}, u32[]{:S(2)}) copy-start(f32[16,1024]{1,0:T(8,128)} %get-tuple-element.18) | copy-start | bytes 196612
  71.3 0.9 %copy-start.1 = (f32[16,1024]{1,0:T(8,128)S(1)}, f32[16,1024]{1,0:T(8,128)}, u32[]{:S(2)}) copy-start(f32[16,1024]{1,0:T(8,128)} %get-tuple-element.11) | copy-start | bytes 196612

commit v3 on v2

v3 whole, which is shorter than its diff:
```python
import jax
import jax.numpy as jnp
from jax import lax
from jax.experimental import pallas as pl
from jax.experimental.pallas import tpu as pltpu
from jax.sharding import PartitionSpec as P

root_half = 0.7071067811865476
inv_root_tau = 0.3989422804014327
F32 = jnp.float32
BF16 = jnp.bfloat16
MESH = pl.DeviceIdType.MESH

ROWS = 512
COLS = 256
D = 1024
UNITS = 1024
NZ, NY = 8, 4
TILE = 256
N_SEM = 99
PHASES = dict(w=0, wc=1, x=2, o=3, g=4, r=5)

NT = (((1,), (1,)), ((), ()))
TN = (((0,), (0,)), ((), ()))


def gelu_pair(pre_act):
    cumul = 0.5 * (1.0 + lax.erf(pre_act * root_half))
    return (pre_act * cumul, cumul + pre_act * jnp.exp(-0.5 * pre_act * pre_act) * inv_root_tau)


def kernel(
    tok_ref, wid_ref, up_ref, down_ref, cot_ref,
    mixed_ref, gtok_ref, gup_ref, gdown_ref,
    uf, vf, xg, hbuf, pbuf, so, ro, fo, perm, permt,
    gsend, grecv, lane, rows_v, wid_v,
    sv, rv, su1, ru1, suz, ruz, svy, rvy, uy, vz,
    ssem, rsem, lsem,
):
    hid = lax.axis_index("hid")
    tok = lax.axis_index("tok")
    c = lax.rem(tok, 2)
    y = lax.rem(lax.div(tok, 2), NY)
    z = lax.div(tok, 2 * NY)

    def zmod(v):
        return lax.rem(v + 2 * NZ, NZ)

    def ymod(v):
        return lax.rem(v + 2 * NY, NY)

    def at(zz, yy, cc):
        return {"tok": (zz * NY + yy) * 2 + cc}

    zp, zm = at(zmod(z + 1), y, c), at(zmod(z - 1), y, c)
    mate = at(z, y, 1 - c)
    near = [at(zmod(z + k), y, c) for k in (1, -1, 2, -2, 3, -3, 4)]
    near += [at(z, ymod(y + r), c) for r in (1, 2, 3)] + [mate]
    xs = [{"hid": lax.rem(hid + k, 4)} for k in (1, 2, 3)]

    slots = {}
    sent = {}

    def slot(table, key):
        return table.setdefault(key, len(table))

    def send(key, src, dst, dev, size=1, phase="w", plane=None):
        sent[phase, plane] = sent.get((phase, plane), 0) + size
        pltpu.make_async_remote_copy(
            src_ref=src, dst_ref=dst, send_sem=ssem.at[PHASES[phase]],
            recv_sem=rsem.at[slot(slots, key)], device_id=dev, device_id_type=MESH,
        ).start()

    def recv(key, size=1):
        part = gsend.at[pl.ds(0, size)]
        pltpu.make_async_remote_copy(
            src_ref=part, dst_ref=part, send_sem=ssem.at[0],
            recv_sem=rsem.at[slot(slots, key)], device_id=mate, device_id_type=MESH,
        ).wait_recv()

    loads = [
        pltpu.make_async_copy(src, dst, lsem.at[i]) for i, (src, dst) in enumerate((
            (up_ref, uf.at[z, y, c]), (down_ref, vf.at[z, y, c]), (wid_ref, wid_v),
            (tok_ref, rows_v.at[0]), (cot_ref, rows_v.at[1]),
        ))
    ]
    for copy in loads:
        copy.start()

    barrier = pltpu.get_barrier_semaphore()
    for dev in near + xs:
        pl.semaphore_signal(barrier, inc=1, device_id=dev, device_id_type=MESH)

    loads[0].wait()
    loads[1].wait()
    pl.semaphore_wait(barrier, len(near) + len(xs))

    def peer_y(r):
        return ymod(y + r)

    def u_share(k):
        zz = zmod(z + k)
        for r in (1, 3, 2):
            ref = uf.at[zz, y, c]
            send(("uy", k), ref, ref, at(z, peer_y(r), c))

    def u_direct(k):
        ref = uf.at[z, y, c]
        send(("uz", k), ref, ref, at(zmod(z + k), y, c))

    def u_pass(k, step):
        ref = uf.at[zmod(z + k), y, c]
        send(("uz", step - k), ref, ref, at(zmod(z + step), y, c))

    def u_recv(k):
        recv(("uz", -k if k != 4 else 4))

    def u_group(k):
        recv(("uy", k), 3)
        zz = zmod(z + k)
        send("wc", uf.at[zz, :, c], uf.at[zz, :, c], mate, 4, "wc")

    def hops(r, d):
        return 4 if (r < 2) == (d == 0) else 3

    def v_send(r, d, s):
        zz = zmod(z - s) if d == 0 else zmod(z + s)
        ref = vf.at[zz, peer_y(r), c]
        send(("vz", r, d, s), ref, ref, zp if d == 0 else zm)

    def v_recv(r, d, s):
        if s < hops(r, d):
            recv(("vz", r, d, s))
            if s + 1 < hops(r, d):
                v_send(r, d, s + 1)

    def v_mate(k):
        zz = zmod(z + k)
        send("wc", vf.at[zz, :, c], vf.at[zz, :, c], mate, 4, "wc")

    own_v = vf.at[z, y, c]
    for r in (1, 3, 2):
        send(("vy", r), own_v, own_v, at(z, peer_y(r), c))
    v_send(0, 0, 0)
    v_send(0, 1, 0)
    u_direct(1)
    u_direct(-1)
    u_share(0)
    u_direct(2)
    u_direct(-2)
    u_direct(4)

    for copy in loads[2:]:
        copy.wait()
    wid = wid_v[...]
    level = lax.broadcasted_iota(jnp.int32, (8, ROWS), 0)
    ind = (jnp.broadcast_to(wid, (8, ROWS)) == level).astype(F32)
    ind16 = ind.astype(BF16)
    ia = lax.broadcasted_iota(jnp.int32, (ROWS, ROWS), 0)
    ib = lax.broadcasted_iota(jnp.int32, (ROWS, ROWS), 1)
    above = (ia < ib).astype(F32).astype(BF16)
    below = (ib < ia).astype(F32).astype(BF16)
    eye = (ia == ib).astype(F32).astype(BF16)
    counts = jnp.sum(ind, axis=1, keepdims=True)
    wider = [
        sum([counts[k:k + 1] for k in range(lo, 4)], jnp.zeros((1, 1), F32)) for lo in range(5)
    ]
    pre_row = jnp.dot(ind16, above, preferred_element_type=F32)
    pre_col = lax.dot_general(below, ind16, NT, preferred_element_type=F32)
    ind_col = lax.dot_general(eye, ind16, NT, preferred_element_type=F32)
    rank_row = sum([ind[k:k + 1] * (pre_row[k:k + 1] + wider[k + 1]) for k in range(4)])
    rank_col = sum(
        [ind_col[:, k:k + 1] * (pre_col[:, k:k + 1] + wider[k + 1]) for k in range(4)]
    )
    perm[...] = (ia == rank_row.astype(jnp.int32)).astype(F32).astype(BF16)
    permt[...] = (ib == rank_col.astype(jnp.int32)).astype(F32).astype(BF16)
    mine = pl.ds(pl.multiple_of(hid * COLS, COLS), COLS)
    for a in (0, 1):
        xg[a, :, mine] = jnp.dot(perm[...], rows_v[a], preferred_element_type=F32).astype(BF16)

    def xpart(h, lo, hi):
        return xg.at[:, pl.ds(lo, hi - lo), pl.ds(h * COLS, COLS)]

    def xsend(src, dst, h, lo, hi, key):
        part = xpart(h, lo, hi)
        send(key, part, part, xs[(dst - src) % 4 - 1], (hi - lo) // 32, "x", src)

    @pl.when(hid == 2)
    def _():
        xsend(2, 1, 2, 0, 128, "x0")
        xsend(2, 3, 2, 128, 256, "x0")
        xsend(2, 3, 2, 0, 64, "xm")
        xsend(2, 1, 2, 256, 384, "x1")
        xsend(2, 3, 2, 384, 512, "x1")

    @pl.when(hid == 1)
    def _():
        xsend(1, 0, 1, 0, 256, "x0")
        xsend(1, 2, 1, 0, 64, "xm")
        xsend(1, 3, 1, 0, 64, "xm")
        xsend(1, 0, 1, 256, 512, "x1")

    @pl.when(hid == 3)
    def _():
        xsend(3, 0, 3, 0, 256, "x0")
        xsend(3, 2, 3, 0, 64, "xm")
        xsend(3, 1, 3, 0, 128, "xm")
        xsend(3, 0, 3, 256, 512, "x1")

    @pl.when(hid == 0)
    def _():
        xsend(0, 1, 0, 0, 128, "xm")
        xsend(0, 3, 0, 0, 64, "xm")
        xsend(0, 2, 0, 0, 64, "xm")

    def forward_tokens(part):
        for plane, lo in ((1, 256 * part), (3, 256 * part + 128)):
            @pl.when(hid == plane)
            def _():
                recv(f"x{part}", 4)
                xsend(plane, 0, 2, lo, lo + 128, f"x{part}")

    for r in (3, 1, 2):
        recv(("vy", (4 - r) % 4))
        v_send(r, 0, 0)
        v_send(r, 1, 0)
    for k in (1, -1):
        u_recv(k)
        u_share(k)
    v_recv(0, 0, 0)
    v_recv(0, 1, 0)
    for k in (2, -2):
        u_recv(k)
        u_pass(k, -1 if k > 0 else 1)
        u_share(k)
    u_recv(4)
    u_share(4)
    forward_tokens(0)
    for r in (3, 1, 2):
        v_recv(r, 0, 0)
        v_recv(r, 1, 0)
    v_mate(0)
    v_mate(-1)
    v_mate(1)
    for k in (3, -3):
        u_recv(k)
        u_share(k)
    u_group(0)
    for r in range(4):
        v_recv(r, 0, 1)
        v_recv(r, 1, 1)
    v_mate(-2)
    v_mate(2)
    u_group(1)
    u_group(-1)
    forward_tokens(1)
    for r in range(4):
        v_recv(r, 0, 2)
        v_recv(r, 1, 2)
    v_mate(-3)
    v_mate(3)
    u_group(2)
    u_group(-2)
    u_group(4)
    for r in range(4):
        v_recv(r, 0, 3)
        v_recv(r, 1, 3)
    v_mate(4)
    u_group(3)
    u_group(-3)
    recv("wc", 64)

    def units(lo_row, n_row, lo_tile, hi_tile, count):
        rows = pl.ds(lo_row, n_row)

        def body(j, carry):
            cols = pl.ds(pl.multiple_of(j * TILE, TILE), TILE)
            u = uf[:, :, :, :, cols].reshape(D, TILE)
            v = vf[:, :, :, :, cols].reshape(D, TILE)
            pre = jnp.dot(xg[0, rows, :], u, preferred_element_type=F32)
            gh = jnp.dot(xg[1, rows, :], v, preferred_element_type=F32)
            act, slope = gelu_pair(pre)
            pg = gh * slope
            if count is not None:
                row = lax.broadcasted_iota(jnp.int32, (n_row, TILE), 0).astype(F32) + lo_row
                keep = row < count
                act = jnp.where(keep, act, 0.0)
                pg = jnp.where(keep, pg, 0.0)
            hbuf[rows, cols] = act.astype(BF16)
            pbuf[rows, cols] = pg.astype(BF16)
            return carry

        lax.fori_loop(lo_tile, hi_tile, body, 0)

    def outputs(plane, d, lo_row, n_row, n_unit):
        rows = pl.ds(lo_row, n_row)
        for a, val, w in ((0, hbuf, vf), (1, pbuf, uf)):
            wt = w[2 * d:2 * d + 2].reshape(COLS, UNITS)[:, :n_unit]
            out = lax.dot_general(val[rows, :n_unit], wt, NT, preferred_element_type=F32)
            if d == plane:
                ro[plane, a, rows, :] = out.astype(BF16)
            else:
                so[d, a, rows, :] = out.astype(BF16)

    def osend(src, dst, d, lo, hi, via=False):
        rows = pl.ds(lo, hi - lo)
        to = fo.at[:, rows, :] if via else ro.at[src, :, rows, :]
        send(f"f{lo // 256}" if via else "o", so.at[d, :, rows, :], to,
             xs[(dst - src) % 4 - 1], (hi - lo) // 32, "o", src)

    def tile(i):
        return lax.rem(lax.div(z, 2) + (2, 1, 3, 0)[i], 4)

    def grads(plane, n_row):
        for i in range(4):
            dt = tile(i)
            cols = pl.ds(pl.multiple_of(dt * COLS, COLS), COLS)
            zs = pl.ds(2 * dt, 2)
            for a, val in ((1, hbuf), (0, pbuf)):
                if plane == 0:
                    left = lax.dot_general(
                        xg[a, :, cols], val[:, :512], TN, preferred_element_type=F32)
                    right = lax.dot_general(
                        xg[a, :256, cols], val[:256, 512:], TN, preferred_element_type=F32)
                    g = jnp.concatenate([left, right], axis=1)
                else:
                    g = lax.dot_general(
                        xg[a, :n_row, cols], val[:n_row, :], TN, preferred_element_type=F32)
                g = g.reshape(2, NY, 2, 16, UNITS)
                lane[a, zs] = jnp.where(c == 0, g[:, :, 0], g[:, :, 1])
                part = pl.ds(32 * a + 8 * dt, 8)
                other = jnp.where(c == 0, g[:, :, 1], g[:, :, 0]).astype(BF16)
                gsend[part] = other.reshape(8, 16, UNITS)
                send(("gc", a, i), gsend.at[part], grecv.at[part], mate, 8, "g", plane)

    def mate_grads(a, tiles):
        for i in tiles:
            recv(("gc", a, i), 8)

    @pl.when(hid == 0)
    def _():
        recv("x0", 24)
        units(0, 256, 0, 2, None)
        units(0, 256, 2, 4, wider[1])
        for d in (2, 1, 3, 0):
            outputs(0, d, 0, 256, 1024)
            if d == 2:
                osend(0, 1, 2, 0, 128, True)
                osend(0, 3, 2, 128, 256, True)
            elif d:
                osend(0, d, d, 0, 256)
        recv("x1", 24)
        units(256, 256, 0, 2, None)
        grads(0, 512)
        for d in (2, 1, 3, 0):
            outputs(0, d, 256, 256, 512)
            if d == 2:
                osend(0, 1, 2, 256, 384, True)
                osend(0, 3, 2, 384, 512, True)
            elif d:
                osend(0, d, d, 256, 512)

    for plane, n_row, n_in, dests in (
        (1, 128, 8, (0, 3, 2, 1)), (2, 64, 6, (0, 1, 3, 2)), (3, 64, 6, (1, 0, 2, 3)),
    ):
        @pl.when(hid == plane)
        def _():
            recv("xm", n_in)
            units(0, n_row, 0, 4, wider[min(plane + 1, 3)])
            for d in dests:
                outputs(plane, d, 0, n_row, 1024)
                if d != plane:
                    osend(plane, d, d, 0, n_row)
            grads(plane, n_row)

    def forward_outputs(part):
        for plane, lo in ((1, 256 * part), (3, 256 * part + 128)):
            @pl.when(hid == plane)
            def _():
                recv(f"f{part}", 4)
                rows = pl.ds(lo, 128)
                send("o", fo.at[:, rows, :], ro.at[0, :, rows, :], xs[(2 - plane) % 4 - 1], 4,
                     "o", plane)

    def total(a, zz, yy):
        return lane[a, zz, yy] + grecv[32 * a + 4 * zz + yy].astype(F32)

    def ring_send(r, d, s):
        zz = zmod(z + 4 - s) if d == 0 else zmod(z - 4 + s)
        val = total(1, zz, peer_y(r))
        if s > 4 - hops(r, d):
            val = val + rv[d, s - 1, r].astype(F32)
        sv[d, s, r] = val.astype(BF16)
        send(("v", r, d, s), sv.at[d, s, r], rv.at[d, s, r], zp if d == 0 else zm, 1, "r")

    def ring_step(s):
        for r in range(4):
            for d in (0, 1):
                if s > 4 - hops(r, d):
                    recv(("v", r, d, s - 1))
                if s >= 4 - hops(r, d):
                    ring_send(r, d, s)

    def up_share(k):
        for r in (1, 3, 2):
            su1[k + 3, r] = total(0, zmod(z + k), peer_y(r)).astype(BF16)
            send(("uu", k), su1.at[k + 3, r], ru1.at[k + 3, r], at(z, peer_y(r), c), 1, "r")

    def up_sum(k):
        val = total(0, zmod(z + k), y)
        recv(("uu", k), 3)
        for r in (1, 3, 2):
            val = val + ru1[k + 3, r].astype(F32)
        return val

    def up_direct(k):
        suz[k + 3] = up_sum(k).astype(BF16)
        send("uw", suz.at[k + 3], ruz.at[k + 3], at(zmod(z + k), y, c), 1, "r")

    mate_grads(1, (0,))
    ring_step(0)
    mate_grads(0, (0,))
    up_share(4)
    mate_grads(1, (1, 2))
    ring_step(1)
    mate_grads(0, (1, 2))
    for k in (3, -3, 2, -2):
        up_share(k)
    forward_outputs(0)
    mate_grads(1, (3,))
    ring_step(2)
    mate_grads(0, (3,))
    for k in (1, -1, 0):
        up_share(k)
    up_direct(4)
    up_direct(3)
    up_direct(-3)
    ring_step(3)
    forward_outputs(1)
    up_direct(2)
    up_direct(-2)
    up_direct(1)
    up_direct(-1)
    uy[...] = up_sum(0)
    for r in (1, 3, 2, 0):
        val = total(1, z, peer_y(r))
        for d in (0, 1):
            recv(("v", r, d, 3))
            val = val + rv[d, 3, r].astype(F32)
        if r:
            svy[r] = val.astype(BF16)
            send("vw", svy.at[r], rvy.at[r], at(z, peer_y(r), c), 1, "r")
        else:
            vz[...] = val

    for plane, n_in in ((0, 8), (1, 20), (2, 22), (3, 22)):
        @pl.when(hid == plane)
        def _():
            recv("o", n_in)

    for a, ref in ((0, mixed_ref), (1, gtok_ref)):
        top = ro[0, a, 0:128].astype(F32) + ro[1, a, 0:128].astype(F32)
        wide = top[:64] + ro[2, a, 0:64].astype(F32) + ro[3, a, 0:64].astype(F32)
        ro[0, a, 0:128] = jnp.concatenate([wide, top[64:]], axis=0).astype(BF16)
        ref[...] = jnp.dot(permt[...], ro[0, a], preferred_element_type=F32).astype(BF16)

    val = vz[...]
    recv("vw", 3)
    for r in (1, 3, 2):
        val = val + rvy[r].astype(F32)
    gdown_ref[...] = val
    val = uy[...]
    recv("uw", 7)
    for k in (4, 3, -3, 2, -2, 1, -1):
        val = val + ruz[k + 3].astype(F32)
    gup_ref[...] = val

    def left(phase, plane):
        part = gsend.at[pl.ds(0, sent[phase, plane])]
        pltpu.make_async_remote_copy(
            src_ref=part, dst_ref=part, send_sem=ssem.at[PHASES[phase]], recv_sem=rsem.at[0],
            device_id=mate, device_id_type=MESH,
        ).wait_send()

    for phase in ("w", "wc", "r"):
        left(phase, None)
    for plane in range(4):
        @pl.when(hid == plane)
        def _():
            for phase in ("x", "o", "g"):
                left(phase, plane)
    assert len(slots) == N_SEM, len(slots)


def store(*refs):
    sem = refs[-1]
    copies = [pltpu.make_async_copy(refs[i], refs[4 + i], sem.at[i]) for i in range(4)]
    for copy in copies:
        copy.start()
    for copy in copies:
        copy.wait()


def per_device(tokens, width_index, up_weight, down_weight, cotangent):
    vm = pl.BlockSpec(memory_space=pltpu.VMEM)
    hbm = pl.BlockSpec(memory_space=pltpu.HBM)
    block = (16, UNITS)
    shapes = [((ROWS, COLS), BF16), ((ROWS, COLS), BF16), (block, F32), (block, F32)]

    def buf(*shape):
        return pltpu.VMEM(shape, BF16)

    results = pl.pallas_call(
        kernel,
        out_shape=tuple(pltpu.VMEM(*shape) for shape in shapes),
        in_specs=[hbm] * 5,
        out_specs=(vm,) * 4,
        scratch_shapes=[
            buf(NZ, NY, 2, *block), buf(NZ, NY, 2, *block),
            buf(2, ROWS, D), buf(ROWS, UNITS), buf(ROWS, UNITS),
            buf(4, 2, ROWS, COLS), buf(4, 2, ROWS, COLS), buf(2, ROWS, COLS),
            buf(ROWS, ROWS), buf(ROWS, ROWS),
            buf(64, *block), buf(64, *block),
            pltpu.VMEM((2, NZ, NY, *block), F32),
            buf(2, ROWS, COLS), pltpu.VMEM((1, ROWS), jnp.int32),
            buf(2, 4, NY, *block), buf(2, 4, NY, *block),
            buf(NZ, NY, *block), buf(NZ, NY, *block),
            buf(NZ, *block), buf(NZ, *block),
            buf(NY, *block), buf(NY, *block),
            pltpu.VMEM(block, F32), pltpu.VMEM(block, F32),
            pltpu.SemaphoreType.DMA((len(PHASES),)), pltpu.SemaphoreType.DMA((N_SEM,)),
            pltpu.SemaphoreType.DMA((5,)),
        ],
        compiler_params=pltpu.CompilerParams(
            collective_id=0, has_side_effects=True, vmem_limit_bytes=48 * 1024 * 1024,
        ),
    )(*[
        pltpu.with_memory_space_constraint(x, pltpu.HBM)
        for x in (tokens, width_index.reshape(1, ROWS), up_weight, down_weight.T, cotangent)
    ])
    mixed, gtok, gup, gdown = pl.pallas_call(
        store,
        out_shape=tuple(jax.ShapeDtypeStruct(*shape) for shape in shapes),
        in_specs=[vm] * 4,
        out_specs=(hbm,) * 4,
        scratch_shapes=[pltpu.SemaphoreType.DMA((4,))],
    )(*[pltpu.with_memory_space_constraint(x, pltpu.VMEM) for x in results])
    return mixed, gtok, gup, gdown.T


def solution(mesh):
    placed = (P("tok", "hid"), P("tok"), P("tok", "hid"), P("hid", "tok"), P("tok", "hid"))
    return jax.shard_map(
        per_device,
        mesh=mesh,
        in_specs=placed,
        out_specs=(P("tok", "hid"), P("tok", "hid"), P("tok", "hid"), P("hid", "tok")),
        check_vma=False,
    )
```

time: 73.1 us -> 64.9 us (0.89)
  Pallas kernels: 68.1 us -> 64 us
  local copies, waits for them, and re-layouts: 4.07 us -> 0 us
    pallas_call x1 -> x2, Pallas kernels: 68.1 us -> 64 us  [the longest x1 63.1 us: per_device(): pl.pallas_call(kernel, out_shape=tuple((pltpu.VMEM(*shape) for shape in s...]
    unnamed x10 -> x0, local copies, waits for them, and re-layouts: 4.07 us -> none
where the time goes in v3:
time: 64.9 us; the launch traced here: 64.8 us
  Pallas kernels  64 us (99%)
  between operations  0.8 us (1%)
    pallas_call x1, Pallas kernels, per_device(): pl.pallas_call(kernel, out_shape=tuple((pltpu.VMEM(*shape) for shape in s...  63.1 us

profile of v3, /device:TPU:1, one launch (start us, length us, event | category | flops | bytes accessed | tf_op | source)
XLA Modules:
  0.0 64.8 jit_solution(14004117403618322585)
XLA Ops:
  0.6 63.1 %shard_map.84 = (bf16[512,256]{1,0:T(8,128)(2,1)S(1)}, bf16[512,256]{1,0:T(8,128)(2,1)S(1)}, f32[16,1024]{1,0:T(8,128)S(1)}, f32[16,1024]{1,0:T(8,128)S(1)}) custom-call(bf16[512,256]{1,0:T(8,128)(2,1)} %tok_ref.1, s32[1,512]{1,0:T(1,128)} %bitcast.4, bf16[16,1024]{1,0:T(8,128)(2,1)} %up_ref.1, bf16[16,1024]{1,0:T(8,128)(2,1)} %bitcast.3, ...), custom_call_target="tpu_custom_call" | custom-call | tf_op jit(solution)/shard_map/pallas_call | solution.py:513
  63.7 0.9 %shard_map.85 = (bf16[512,256]{1,0:T(8,128)(2,1)}, bf16[512,256]{1,0:T(8,128)(2,1)}, f32[16,1024]{1,0:T(8,128)}, f32[16,1024]{1,0:T(8,128)}) custom-call(bf16[512,256]{1,0:T(8,128)(2,1)S(1)} %get-tuple-element.12.refs_0_, bf16[512,256]{1,0:T(8,128)(2,1)S(1)} %get-tuple-element.13.refs_1_, f32[16,1024]{1,0:T(8,128)S(1)} %get-tuple-element.14.refs_2_, ...), custom_call_target="tpu_custom_call" | custom-call | tf_op jit(solution)/shard_map/pallas_call | solution.py:541

commit v4 on v3

--- a/solution.py
+++ b/solution.py
@@ -17,7 +17,9 @@
 UNITS = 1024
 NZ, NY = 8, 4
 TILE = 256
-N_SEM = 99
+HALF = 512
+N_SEM = 119
+GROUP = (0, 1, 1, 2)
 PHASES = dict(w=0, wc=1, x=2, o=3, g=4, r=5)
 
 NT = (((1,), (1,)), ((), ()))
@@ -49,14 +51,22 @@
     def ymod(v):
         return lax.rem(v + 2 * NY, NY)
 
+    def halves(h):
+        return pl.ds(HALF * h, HALF)
+
     def at(zz, yy, cc):
         return {"tok": (zz * NY + yy) * 2 + cc}
 
     zp, zm = at(zmod(z + 1), y, c), at(zmod(z - 1), y, c)
     mate = at(z, y, 1 - c)
-    near = [at(zmod(z + k), y, c) for k in (1, -1, 2, -2, 3, -3, 4)]
+    near = [at(zmod(z + k), y, c) for k in (1, -1, 2, -2)]
     near += [at(z, ymod(y + r), c) for r in (1, 2, 3)] + [mate]
     xs = [{"hid": lax.rem(hid + k, 4)} for k in (1, 2, 3)]
+
+    def stand_in(size):
+        if size == int(size):
+            return gsend.at[pl.ds(0, int(size))]
+        return gsend.at[pl.ds(0, int(2 * size)), :, pl.ds(0, HALF)]
 
     slots = {}
     sent = {}
@@ -72,7 +82,7 @@
         ).start()
 
     def recv(key, size=1):
-        part = gsend.at[pl.ds(0, size)]
+        part = stand_in(size)
         pltpu.make_async_remote_copy(
             src_ref=part, dst_ref=part, send_sem=ssem.at[0],
             recv_sem=rsem.at[slot(slots, key)], device_id=mate, device_id_type=MESH,
@@ -108,9 +118,12 @@
         ref = uf.at[z, y, c]
         send(("uz", k), ref, ref, at(zmod(z + k), y, c))
 
-    def u_pass(k, step):
+    def u_pass(k):
+        near, far, cols = (-1, -2, halves(1)) if k > 0 else (1, 2, halves(0))
         ref = uf.at[zmod(z + k), y, c]
-        send(("uz", step - k), ref, ref, at(zmod(z + step), y, c))
+        send(("uz", near - k), ref, ref, at(zmod(z + near), y, c))
+        ref = uf.at[zmod(z + k), y, c, :, cols]
+        send(("uz", 4), ref, ref, at(zmod(z + far), y, c), 0.5)
 
     def u_recv(k):
         recv(("uz", -k if k != 4 else 4))
@@ -127,16 +140,17 @@
         zz = zmod(z - s) if d == 0 else zmod(z + s)
         ref = vf.at[zz, peer_y(r), c]
         send(("vz", r, d, s), ref, ref, zp if d == 0 else zm)
+
+    def v_mate(r, zz):
+        ref = vf.at[zz, peer_y(r), c]
+        send("wc", ref, ref, mate, 1, "wc")
 
     def v_recv(r, d, s):
         if s < hops(r, d):
             recv(("vz", r, d, s))
             if s + 1 < hops(r, d):
                 v_send(r, d, s + 1)
-
-    def v_mate(k):
-        zz = zmod(z + k)
-        send("wc", vf.at[zz, :, c], vf.at[zz, :, c], mate, 4, "wc")
+            v_mate(r, zmod(z - s - 1) if d == 0 else zmod(z + s + 1))
 
     own_v = vf.at[z, y, c]
     for r in (1, 3, 2):
@@ -148,7 +162,6 @@
     u_share(0)
     u_direct(2)
     u_direct(-2)
-    u_direct(4)
 
     for copy in loads[2:]:
         copy.wait()
@@ -224,6 +237,8 @@
         recv(("vy", (4 - r) % 4))
         v_send(r, 0, 0)
         v_send(r, 1, 0)
+        v_mate(r, z)
+    v_mate(0, z)
     for k in (1, -1):
         u_recv(k)
         u_share(k)
@@ -231,43 +246,33 @@
     v_recv(0, 1, 0)
     for k in (2, -2):
         u_recv(k)
-        u_pass(k, -1 if k > 0 else 1)
+        u_pass(k)
         u_share(k)
-    u_recv(4)
-    u_share(4)
     forward_tokens(0)
     for r in (3, 1, 2):
         v_recv(r, 0, 0)
         v_recv(r, 1, 0)
-    v_mate(0)
-    v_mate(-1)
-    v_mate(1)
-    for k in (3, -3):
+    for k in (3, -3, 4):
         u_recv(k)
         u_share(k)
     u_group(0)
     for r in range(4):
         v_recv(r, 0, 1)
         v_recv(r, 1, 1)
-    v_mate(-2)
-    v_mate(2)
     u_group(1)
     u_group(-1)
     forward_tokens(1)
     for r in range(4):
         v_recv(r, 0, 2)
         v_recv(r, 1, 2)
-    v_mate(-3)
-    v_mate(3)
     u_group(2)
     u_group(-2)
-    u_group(4)
     for r in range(4):
         v_recv(r, 0, 3)
         v_recv(r, 1, 3)
-    v_mate(4)
     u_group(3)
     u_group(-3)
+    u_group(4)
     recv("wc", 64)
 
     def units(lo_row, n_row, lo_tile, hi_tile, count):
@@ -311,67 +316,71 @@
     def tile(i):
         return lax.rem(lax.div(z, 2) + (2, 1, 3, 0)[i], 4)
 
-    def grads(plane, n_row):
+    def grads(plane, n_row, h):
+        hc = halves(h)
         for i in range(4):
             dt = tile(i)
             cols = pl.ds(pl.multiple_of(dt * COLS, COLS), COLS)
             zs = pl.ds(2 * dt, 2)
             for a, val in ((1, hbuf), (0, pbuf)):
-                if plane == 0:
-                    left = lax.dot_general(
-                        xg[a, :, cols], val[:, :512], TN, preferred_element_type=F32)
-                    right = lax.dot_general(
-                        xg[a, :256, cols], val[:256, 512:], TN, preferred_element_type=F32)
-                    g = jnp.concatenate([left, right], axis=1)
-                else:
-                    g = lax.dot_general(
-                        xg[a, :n_row, cols], val[:n_row, :], TN, preferred_element_type=F32)
-                g = g.reshape(2, NY, 2, 16, UNITS)
-                lane[a, zs] = jnp.where(c == 0, g[:, :, 0], g[:, :, 1])
+                g = lax.dot_general(
+                    xg[a, :n_row, cols], val[:n_row, hc], TN, preferred_element_type=F32)
+                g = g.reshape(2, NY, 2, 16, HALF)
+                lane[a, zs, :, :, hc] = jnp.where(c == 0, g[:, :, 0], g[:, :, 1])
                 part = pl.ds(32 * a + 8 * dt, 8)
                 other = jnp.where(c == 0, g[:, :, 1], g[:, :, 0]).astype(BF16)
-                gsend[part] = other.reshape(8, 16, UNITS)
-                send(("gc", a, i), gsend.at[part], grecv.at[part], mate, 8, "g", plane)
-
-    def mate_grads(a, tiles):
-        for i in tiles:
-            recv(("gc", a, i), 8)
+                gsend[part, :, hc] = other.reshape(8, 16, HALF)
+                send(("gc", h, a, GROUP[i]), gsend.at[part, :, hc], grecv.at[part, :, hc], mate,
+                     4, "g", plane)
+
+    def mate_grads(h, a, group):
+        recv(("gc", h, a, group), 8 if group == 1 else 4)
+
+    others = (
+        (1, 128, 8, (0, 3, 2, 1)), (2, 64, 6, (0, 1, 3, 2)), (3, 64, 6, (1, 0, 2, 3)),
+    )
+
+    def row_outputs(lo, n_unit):
+        for d in (2, 1, 3, 0):
+            outputs(0, d, lo, 256, n_unit)
+            if d == 2:
+                osend(0, 1, 2, lo, lo + 128, True)
+                osend(0, 3, 2, lo + 128, lo + 256, True)
+            elif d:
+                osend(0, d, d, lo, lo + 256)
 
     @pl.when(hid == 0)
     def _():
         recv("x0", 24)
+        units(0, 256, 2, 4, wider[1])
+        grads(0, 256, 1)
         units(0, 256, 0, 2, None)
-        units(0, 256, 2, 4, wider[1])
-        for d in (2, 1, 3, 0):
-            outputs(0, d, 0, 256, 1024)
-            if d == 2:
-                osend(0, 1, 2, 0, 128, True)
-                osend(0, 3, 2, 128, 256, True)
-            elif d:
-                osend(0, d, d, 0, 256)
-        recv("x1", 24)
-        units(256, 256, 0, 2, None)
-        grads(0, 512)
-        for d in (2, 1, 3, 0):
-            outputs(0, d, 256, 256, 512)
-            if d == 2:
-                osend(0, 1, 2, 256, 384, True)
-                osend(0, 3, 2, 384, 512, True)
-            elif d:
-                osend(0, d, d, 256, 512)
-
-    for plane, n_row, n_in, dests in (
-        (1, 128, 8, (0, 3, 2, 1)), (2, 64, 6, (0, 1, 3, 2)), (3, 64, 6, (1, 0, 2, 3)),
-    ):
+
+    for plane, n_row, n_in, dests in others:
         @pl.when(hid == plane)
         def _():
             recv("xm", n_in)
-            units(0, n_row, 0, 4, wider[min(plane + 1, 3)])
+            count = wider[min(plane + 1, 3)]
+            units(0, n_row, 2, 4, count)
+            grads(plane, n_row, 1)
+            units(0, n_row, 0, 2, count)
             for d in dests:
-                outputs(plane, d, 0, n_row, 1024)
+                outputs(plane, d, 0, n_row, UNITS)
                 if d != plane:
                     osend(plane, d, d, 0, n_row)
-            grads(plane, n_row)
+
+    def rest_of_rows():
+        @pl.when(hid == 0)
+        def _():
+            recv("x1", 24)
+            units(256, 256, 0, 2, None)
+            grads(0, 512, 0)
+            row_outputs(0, UNITS)
+
+        for plane, n_row, _, _ in others:
+            @pl.when(hid == plane)
+            def _():
+                grads(plane, n_row, 0)
 
     def forward_outputs(part):
         for plane, lo in ((1, 256 * part), (3, 256 * part + 128)):
@@ -382,76 +391,128 @@
                 send("o", fo.at[:, rows, :], ro.at[0, :, rows, :], xs[(2 - plane) % 4 - 1], 4,
                      "o", plane)
 
-    def total(a, zz, yy):
-        return lane[a, zz, yy] + grecv[32 * a + 4 * zz + yy].astype(F32)
-
-    def ring_send(r, d, s):
-        zz = zmod(z + 4 - s) if d == 0 else zmod(z - 4 + s)
-        val = total(1, zz, peer_y(r))
-        if s > 4 - hops(r, d):
-            val = val + rv[d, s - 1, r].astype(F32)
-        sv[d, s, r] = val.astype(BF16)
-        send(("v", r, d, s), sv.at[d, s, r], rv.at[d, s, r], zp if d == 0 else zm, 1, "r")
-
-    def ring_step(s):
-        for r in range(4):
+    def total(h, a, zz, yy):
+        hc = halves(h)
+        return lane[a, zz, yy, :, hc] + grecv[32 * a + 4 * zz + yy, :, hc].astype(F32)
+
+    def steps(p, d):
+        return 4 if p == d else 3
+
+    def ring(h, s):
+        hc = halves(h)
+        for p in (0, 1):
             for d in (0, 1):
-                if s > 4 - hops(r, d):
-                    recv(("v", r, d, s - 1))
-                if s >= 4 - hops(r, d):
-                    ring_send(r, d, s)
-
-    def up_share(k):
+                first = 4 - steps(p, d)
+                ys = pl.ds(2 * p, 2)
+                if s > first:
+                    recv(("v", h, p, d, s - 1))
+                if s < first:
+                    continue
+                zz = zmod(z + 4 - s) if d == 0 else zmod(z - 4 + s)
+                for r in (2 * p, 2 * p + 1):
+                    val = total(h, 1, zz, peer_y(r))
+                    if s > first:
+                        val = val + rv[d, s - 1, r, :, hc].astype(F32)
+                    sv[d, s, r, :, hc] = val.astype(BF16)
+                send(("v", h, p, d, s), sv.at[d, s, ys, :, hc], rv.at[d, s, ys, :, hc],
+                     zp if d == 0 else zm, 1, "r")
+
+    def ring_end(h):
+        hc = halves(h)
+        for p in (1, 0):
+            for d in (0, 1):
+                recv(("v", h, p, d, 3))
+            for r in (2 * p + 1, 2 * p):
+                val = total(h, 1, z, peer_y(r))
+                for d in (0, 1):
+                    val = val + rv[d, 3, r, :, hc].astype(F32)
+                if r:
+                    svy[r, :, hc] = val.astype(BF16)
+                    send(("vw", h), svy.at[r, :, hc], rvy.at[r, :, hc], at(z, peer_y(r), c),
+                         0.5, "r")
+                else:
+                    vz[:, hc] = val
+
+    def up_share(h, k):
+        hc = halves(h)
         for r in (1, 3, 2):
-            su1[k + 3, r] = total(0, zmod(z + k), peer_y(r)).astype(BF16)
-            send(("uu", k), su1.at[k + 3, r], ru1.at[k + 3, r], at(z, peer_y(r), c), 1, "r")
-
-    def up_sum(k):
-        val = total(0, zmod(z + k), y)
-        recv(("uu", k), 3)
+            su1[k + 3, r, :, hc] = total(h, 0, zmod(z + k), peer_y(r)).astype(BF16)
+            send(("uu", h, k), su1.at[k + 3, r, :, hc], ru1.at[k + 3, r, :, hc],
+                 at(z, peer_y(r), c), 0.5, "r")
+
+    def up_sum(h, k):
+        hc = halves(h)
+        val = total(h, 0, zmod(z + k), y)
+        recv(("uu", h, k), 1.5)
         for r in (1, 3, 2):
-            val = val + ru1[k + 3, r].astype(F32)
+            val = val + ru1[k + 3, r, :, hc].astype(F32)
         return val
 
-    def up_direct(k):
-        suz[k + 3] = up_sum(k).astype(BF16)
-        send("uw", suz.at[k + 3], ruz.at[k + 3], at(zmod(z + k), y, c), 1, "r")
-
-    mate_grads(1, (0,))
-    ring_step(0)
-    mate_grads(0, (0,))
-    up_share(4)
-    mate_grads(1, (1, 2))
-    ring_step(1)
-    mate_grads(0, (1, 2))
-    for k in (3, -3, 2, -2):
-        up_share(k)
+    def up_send(h, k, val, key, hop):
+        hc = halves(h)
+        suz[k + 3, :, hc] = val.astype(BF16)
+        send(key, suz.at[k + 3, :, hc], ruz.at[k + 3, :, hc], at(zmod(z + hop), y, c), 0.5, "r")
+
+    def up_far(h):
+        up_send(h, 4, up_sum(h, 4), ("uf", h, 4), 2 if h == 0 else -2)
+        up_send(h, 3, up_sum(h, 3), ("uf", h, 3), 1)
+        up_send(h, -3, up_sum(h, -3), ("uf", h, -3), -1)
+
+    def up_near(h):
+        for k in (1, -1):
+            up_send(h, k, up_sum(h, k), ("ue", h), k)
+
+    def up_two(h):
+        hc = halves(h)
+        for k, far in ((2, 3), (-2, -3)):
+            val = up_sum(h, k)
+            recv(("uf", h, far), 0.5)
+            val = val + ruz[far + 3, :, hc].astype(F32)
+            if (k == 2) == (h == 0):
+                recv(("uf", h, 4), 0.5)
+                val = val + ruz[7, :, hc].astype(F32)
+            up_send(h, k, val, ("ue", h), k)
+
+    def start_half(h):
+        mate_grads(h, 1, 0)
+        ring(h, 0)
+        mate_grads(h, 0, 0)
+        up_share(h, 4)
+        mate_grads(h, 0, 1)
+        for k in (3, -3, 2, -2):
+            up_share(h, k)
+        mate_grads(h, 0, 2)
+        for k in (1, -1, 0):
+            up_share(h, k)
+        mate_grads(h, 1, 1)
+        mate_grads(h, 1, 2)
+
+    start_half(1)
+    rest_of_rows()
+    start_half(0)
+    ring(1, 1)
+    up_far(1)
+
+    @pl.when(hid == 0)
+    def _():
+        row_outputs(256, HALF)
+
+    ring(0, 1)
+    ring(1, 2)
+    up_near(1)
+    up_far(0)
     forward_outputs(0)
-    mate_grads(1, (3,))
-    ring_step(2)
-    mate_grads(0, (3,))
-    for k in (1, -1, 0):
-        up_share(k)
-    up_direct(4)
-    up_direct(3)
-    up_direct(-3)
-    ring_step(3)
+    ring(0, 2)
+    ring(1, 3)
+    up_two(1)
+    up_near(0)
+    ring(0, 3)
+    ring_end(1)
+    uy[:, halves(1)] = up_sum(1, 0)
+    up_two(0)
     forward_outputs(1)
-    up_direct(2)
-    up_direct(-2)
-    up_direct(1)
-    up_direct(-1)
-    uy[...] = up_sum(0)
-    for r in (1, 3, 2, 0):
-        val = total(1, z, peer_y(r))
-        for d in (0, 1):
-            recv(("v", r, d, 3))
-            val = val + rv[d, 3, r].astype(F32)
-        if r:
-            svy[r] = val.astype(BF16)
-            send("vw", svy.at[r], rvy.at[r], at(z, peer_y(r), c), 1, "r")
-        else:
-            vz[...] = val
+    uy[:, halves(0)] = up_sum(0, 0)
+    ring_end(0)
 
     for plane, n_in in ((0, 8), (1, 20), (2, 22), (3, 22)):
         @pl.when(hid == plane)
@@ -464,19 +525,21 @@
         ro[0, a, 0:128] = jnp.concatenate([wide, top[64:]], axis=0).astype(BF16)
         ref[...] = jnp.dot(permt[...], ro[0, a], preferred_element_type=F32).astype(BF16)
 
-    val = vz[...]
-    recv("vw", 3)
-    for r in (1, 3, 2):
-        val = val + rvy[r].astype(F32)
-    gdown_ref[...] = val
-    val = uy[...]
-    recv("uw", 7)
-    for k in (4, 3, -3, 2, -2, 1, -1):
-        val = val + ruz[k + 3].astype(F32)
-    gup_ref[...] = val
+    for h in (1, 0):
+        hc = halves(h)
+        recv(("vw", h), 1.5)
+        val = vz[:, hc]
+        for r in (1, 3, 2):
+            val = val + rvy[r, :, hc].astype(F32)
+        gdown_ref[:, hc] = val
+        recv(("ue", h), 2)
+        val = uy[:, hc]
+        for k in (1, -1, 2, -2):
+            val = val + ruz[k + 3, :, hc].astype(F32)
+        gup_ref[:, hc] = val
 
     def left(phase, plane):
-        part = gsend.at[pl.ds(0, sent[phase, plane])]
+        part = stand_in(sent[phase, plane])
         pltpu.make_async_remote_copy(
             src_ref=part, dst_ref=part, send_sem=ssem.at[PHASES[phase]], recv_sem=rsem.at[0],
             device_id=mate, device_id_type=MESH,

time: 64.9 us -> 61.6 us (0.949)
  Pallas kernels: 64 us -> 60.2 us
    pallas_call x1, Pallas kernels: 63.1 us -> 59.4 us  [per_device(): pl.pallas_call(kernel, out_shape=tuple((pltpu.VMEM(*shape) for shape in s...]
where the time goes in v4:
time: 61.6 us; the launch traced here: 61 us
  Pallas kernels  60.2 us (98%)
  between operations  0.8 us (1%)
    pallas_call x1, Pallas kernels, per_device(): pl.pallas_call(kernel, out_shape=tuple((pltpu.VMEM(*shape) for shape in s...  59.4 us

profile of v4, /device:TPU:1, one launch (start us, length us, event | category | flops | bytes accessed | tf_op | source)
XLA Modules:
  0.0 61.0 jit_solution(10359839978183027978)
XLA Ops:
  0.6 59.4 %shard_map.84 = (bf16[512,256]{1,0:T(8,128)(2,1)S(1)}, bf16[512,256]{1,0:T(8,128)(2,1)S(1)}, f32[16,1024]{1,0:T(8,128)S(1)}, f32[16,1024]{1,0:T(8,128)S(1)}) custom-call(bf16[512,256]{1,0:T(8,128)(2,1)} %tok_ref.1, s32[1,512]{1,0:T(1,128)} %bitcast.4, bf16[16,1024]{1,0:T(8,128)(2,1)} %up_ref.1, bf16[16,1024]{1,0:T(8,128)(2,1)} %bitcast.3, ...), custom_call_target="tpu_custom_call" | custom-call | tf_op jit(solution)/shard_map/pallas_call | solution.py:576
  60.0 0.9 %shard_map.85 = (bf16[512,256]{1,0:T(8,128)(2,1)}, bf16[512,256]{1,0:T(8,128)(2,1)}, f32[16,1024]{1,0:T(8,128)}, f32[16,1024]{1,0:T(8,128)}) custom-call(bf16[512,256]{1,0:T(8,128)(2,1)S(1)} %get-tuple-element.12.refs_0_, bf16[512,256]{1,0:T(8,128)(2,1)S(1)} %get-tuple-element.13.refs_1_, f32[16,1024]{1,0:T(8,128)S(1)} %get-tuple-element.14.refs_2_, ...), custom_call_target="tpu_custom_call" | custom-call | tf_op jit(solution)/shard_map/pallas_call | solution.py:604

commit v5 on v4

--- a/solution.py
+++ b/solution.py
@@ -133,30 +133,32 @@
         zz = zmod(z + k)
         send("wc", uf.at[zz, :, c], uf.at[zz, :, c], mate, 4, "wc")
 
-    def hops(r, d):
-        return 4 if (r < 2) == (d == 0) else 3
-
-    def v_send(r, d, s):
-        zz = zmod(z - s) if d == 0 else zmod(z + s)
-        ref = vf.at[zz, peer_y(r), c]
-        send(("vz", r, d, s), ref, ref, zp if d == 0 else zm)
-
-    def v_mate(r, zz):
-        ref = vf.at[zz, peer_y(r), c]
+    def v_mate(r, k):
+        ref = vf.at[zmod(z + k), peer_y(r), c]
         send("wc", ref, ref, mate, 1, "wc")
 
-    def v_recv(r, d, s):
-        if s < hops(r, d):
-            recv(("vz", r, d, s))
-            if s + 1 < hops(r, d):
-                v_send(r, d, s + 1)
-            v_mate(r, zmod(z - s - 1) if d == 0 else zmod(z + s + 1))
+    def v_to(r, k, hop):
+        ref = vf.at[zmod(z + k), peer_y(r), c]
+        far = k - hop
+        send(("vz", r, 4 if abs(far) == 4 else far), ref, ref, at(zmod(z + hop), y, c))
+
+    def v_direct(r):
+        for k in (1, -1, 2, -2):
+            v_to(r, 0, k)
+
+    def v_recv(r, k):
+        recv(("vz", r, k))
+        if abs(k) == 2:
+            near = -1 if k > 0 else 1
+            if (r < 2) == (k < 0):
+                v_to(r, k, 2 * near)
+            v_to(r, k, near)
+        v_mate(r, k)
 
     own_v = vf.at[z, y, c]
     for r in (1, 3, 2):
         send(("vy", r), own_v, own_v, at(z, peer_y(r), c))
-    v_send(0, 0, 0)
-    v_send(0, 1, 0)
+    v_direct(0)
     u_direct(1)
     u_direct(-1)
     u_share(0)
@@ -235,41 +237,36 @@
 
     for r in (3, 1, 2):
         recv(("vy", (4 - r) % 4))
-        v_send(r, 0, 0)
-        v_send(r, 1, 0)
-        v_mate(r, z)
-    v_mate(0, z)
+        v_direct(r)
+        v_mate(r, 0)
+    v_mate(0, 0)
     for k in (1, -1):
         u_recv(k)
         u_share(k)
-    v_recv(0, 0, 0)
-    v_recv(0, 1, 0)
     for k in (2, -2):
         u_recv(k)
         u_pass(k)
         u_share(k)
+    for k in (2, -2, 1, -1):
+        v_recv(0, k)
     forward_tokens(0)
     for r in (3, 1, 2):
-        v_recv(r, 0, 0)
-        v_recv(r, 1, 0)
+        for k in (2, -2, 1, -1):
+            v_recv(r, k)
     for k in (3, -3, 4):
         u_recv(k)
         u_share(k)
     u_group(0)
-    for r in range(4):
-        v_recv(r, 0, 1)
-        v_recv(r, 1, 1)
+    for k in (3, -3, 4):
+        v_recv(0, k)
     u_group(1)
     u_group(-1)
     forward_tokens(1)
-    for r in range(4):
-        v_recv(r, 0, 2)
-        v_recv(r, 1, 2)
     u_group(2)
     u_group(-2)
-    for r in range(4):
-        v_recv(r, 0, 3)
-        v_recv(r, 1, 3)
+    for r in (3, 1, 2):
+        for k in (3, -3, 4):
+            v_recv(r, k)
     u_group(3)
     u_group(-3)
     u_group(4)
@@ -295,7 +292,7 @@
             pbuf[rows, cols] = pg.astype(BF16)
             return carry
 
-        lax.fori_loop(lo_tile, hi_tile, body, 0)
+        lax.fori_loop(lo_tile, hi_tile, body, 0, unroll=True)
 
     def outputs(plane, d, lo_row, n_row, n_unit):
         rows = pl.ds(lo_row, n_row)
@@ -340,8 +337,8 @@
         (1, 128, 8, (0, 3, 2, 1)), (2, 64, 6, (0, 1, 3, 2)), (3, 64, 6, (1, 0, 2, 3)),
     )
 
-    def row_outputs(lo, n_unit):
-        for d in (2, 1, 3, 0):
+    def row_outputs(lo, n_unit, dests=(2, 1, 3, 0)):
+        for d in dests:
             outputs(0, d, lo, 256, n_unit)
             if d == 2:
                 osend(0, 1, 2, lo, lo + 128, True)
@@ -373,9 +370,11 @@
         @pl.when(hid == 0)
         def _():
             recv("x1", 24)
+            row_outputs(0, UNITS, (2,))
             units(256, 256, 0, 2, None)
+            row_outputs(0, UNITS, (1, 3))
             grads(0, 512, 0)
-            row_outputs(0, UNITS)
+            row_outputs(0, UNITS, (0,))
 
         for plane, n_row, _, _ in others:
             @pl.when(hid == plane)

time: 61.6 us -> 60.1 us (0.976)
  Pallas kernels: 60.2 us -> 59.2 us
    pallas_call x1, Pallas kernels: 59.4 us -> 58.4 us  [per_device(): pl.pallas_call(kernel, out_shape=tuple((pltpu.VMEM(*shape) for shape in s...]
where the time goes in v5:
time: 60.1 us; the launch traced here: 60 us
  Pallas kernels  59.2 us (99%)
  between operations  0.8 us (1%)
    pallas_call x1, Pallas kernels, per_device(): pl.pallas_call(kernel, out_shape=tuple((pltpu.VMEM(*shape) for shape in s...  58.4 us

profile of v5, /device:TPU:1, one launch (start us, length us, event | category | flops | bytes accessed | tf_op | source)
XLA Modules:
  0.0 60.0 jit_solution(12684498819780164305)
XLA Ops:
  0.6 58.4 %shard_map.84 = (bf16[512,256]{1,0:T(8,128)(2,1)S(1)}, bf16[512,256]{1,0:T(8,128)(2,1)S(1)}, f32[16,1024]{1,0:T(8,128)S(1)}, f32[16,1024]{1,0:T(8,128)S(1)}) custom-call(bf16[512,256]{1,0:T(8,128)(2,1)} %tok_ref.1, s32[1,512]{1,0:T(1,128)} %bitcast.4, bf16[16,1024]{1,0:T(8,128)(2,1)} %up_ref.1, bf16[16,1024]{1,0:T(8,128)(2,1)} %bitcast.3, ...), custom_call_target="tpu_custom_call" | custom-call | tf_op jit(solution)/shard_map/pallas_call | solution.py:575
  59.0 0.9 %shard_map.85 = (bf16[512,256]{1,0:T(8,128)(2,1)}, bf16[512,256]{1,0:T(8,128)(2,1)}, f32[16,1024]{1,0:T(8,128)}, f32[16,1024]{1,0:T(8,128)}) custom-call(bf16[512,256]{1,0:T(8,128)(2,1)S(1)} %get-tuple-element.12.refs_0_, bf16[512,256]{1,0:T(8,128)(2,1)S(1)} %get-tuple-element.13.refs_1_, f32[16,1024]{1,0:T(8,128)S(1)} %get-tuple-element.14.refs_2_, ...), custom_call_target="tpu_custom_call" | custom-call | tf_op jit(solution)/shard_map/pallas_call | solution.py:603

commit v6 on v5

--- a/solution.py
+++ b/solution.py
@@ -352,6 +352,7 @@
         units(0, 256, 2, 4, wider[1])
         grads(0, 256, 1)
         units(0, 256, 0, 2, None)
+        row_outputs(0, UNITS, (2,))
 
     for plane, n_row, n_in, dests in others:
         @pl.when(hid == plane)
@@ -370,7 +371,6 @@
         @pl.when(hid == 0)
         def _():
             recv("x1", 24)
-            row_outputs(0, UNITS, (2,))
             units(256, 256, 0, 2, None)
             row_outputs(0, UNITS, (1, 3))
             grads(0, 512, 0)

time: 60.1 us -> 59.9 us (level)
  no operation moved by 1% of the time
where the time goes in v6:
time: 59.9 us; the launch traced here: 59.8 us
  Pallas kernels  59 us (98%)
  between operations  0.8 us (1%)
    pallas_call x1, Pallas kernels, per_device(): pl.pallas_call(kernel, out_shape=tuple((pltpu.VMEM(*shape) for shape in s...  58.1 us

profile of v6, /device:TPU:1, one launch (start us, length us, event | category | flops | bytes accessed | tf_op | source)
XLA Modules:
  0.0 59.8 jit_solution(17634894606280375568)
XLA Ops:
  0.6 58.1 %shard_map.84 = (bf16[512,256]{1,0:T(8,128)(2,1)S(1)}, bf16[512,256]{1,0:T(8,128)(2,1)S(1)}, f32[16,1024]{1,0:T(8,128)S(1)}, f32[16,1024]{1,0:T(8,128)S(1)}) custom-call(bf16[512,256]{1,0:T(8,128)(2,1)} %tok_ref.1, s32[1,512]{1,0:T(1,128)} %bitcast.4, bf16[16,1024]{1,0:T(8,128)(2,1)} %up_ref.1, bf16[16,1024]{1,0:T(8,128)(2,1)} %bitcast.3, ...), custom_call_target="tpu_custom_call" | custom-call | tf_op jit(solution)/shard_map/pallas_call | solution.py:575
  58.8 0.9 %shard_map.85 = (bf16[512,256]{1,0:T(8,128)(2,1)}, bf16[512,256]{1,0:T(8,128)(2,1)}, f32[16,1024]{1,0:T(8,128)}, f32[16,1024]{1,0:T(8,128)}) custom-call(bf16[512,256]{1,0:T(8,128)(2,1)S(1)} %get-tuple-element.12.refs_0_, bf16[512,256]{1,0:T(8,128)(2,1)S(1)} %get-tuple-element.13.refs_1_, f32[16,1024]{1,0:T(8,128)S(1)} %get-tuple-element.14.refs_2_, ...), custom_call_target="tpu_custom_call" | custom-call | tf_op jit(solution)/shard_map/pallas_call | solution.py:603

commit v7 on v6

--- a/solution.py
+++ b/solution.py
@@ -372,9 +372,8 @@
         def _():
             recv("x1", 24)
             units(256, 256, 0, 2, None)
-            row_outputs(0, UNITS, (1, 3))
             grads(0, 512, 0)
-            row_outputs(0, UNITS, (0,))
+            row_outputs(0, UNITS, (1, 3, 0))
 
         for plane, n_row, _, _ in others:
             @pl.when(hid == plane)

time: 59.9 us -> 60.3 us (level)
  no operation moved by 1% of the time
where the time goes in v7:
time: 60.3 us; the launch traced here: 60.2 us
  Pallas kernels  59.4 us (99%)
  between operations  0.8 us (1%)
    pallas_call x1, Pallas kernels, per_device(): pl.pallas_call(kernel, out_shape=tuple((pltpu.VMEM(*shape) for shape in s...  58.5 us

profile of v7, /device:TPU:1, one launch (start us, length us, event | category | flops | bytes accessed | tf_op | source)
XLA Modules:
  0.0 60.2 jit_solution(15864915897406625633)
XLA Ops:
  0.6 58.5 %shard_map.84 = (bf16[512,256]{1,0:T(8,128)(2,1)S(1)}, bf16[512,256]{1,0:T(8,128)(2,1)S(1)}, f32[16,1024]{1,0:T(8,128)S(1)}, f32[16,1024]{1,0:T(8,128)S(1)}) custom-call(bf16[512,256]{1,0:T(8,128)(2,1)} %tok_ref.1, s32[1,512]{1,0:T(1,128)} %bitcast.4, bf16[16,1024]{1,0:T(8,128)(2,1)} %up_ref.1, bf16[16,1024]{1,0:T(8,128)(2,1)} %bitcast.3, ...), custom_call_target="tpu_custom_call" | custom-call | tf_op jit(solution)/shard_map/pallas_call | solution.py:574
  59.2 0.9 %shard_map.85 = (bf16[512,256]{1,0:T(8,128)(2,1)}, bf16[512,256]{1,0:T(8,128)(2,1)}, f32[16,1024]{1,0:T(8,128)}, f32[16,1024]{1,0:T(8,128)}) custom-call(bf16[512,256]{1,0:T(8,128)(2,1)S(1)} %get-tuple-element.12.refs_0_, bf16[512,256]{1,0:T(8,128)(2,1)S(1)} %get-tuple-element.13.refs_1_, f32[16,1024]{1,0:T(8,128)S(1)} %get-tuple-element.14.refs_2_, ...), custom_call_target="tpu_custom_call" | custom-call | tf_op jit(solution)/shard_map/pallas_call | solution.py:602
